TPU v7x, 32 devices: a whole 2x2x4 slice. The times are simulated.
32 devices in a mesh: wide: 8 (over z, x), narrow: 4 (over y, core).
Axes of the slice: x: 2, y: 2, z: 4, core: 2. Of those that a mesh axis runs over, the one named last changes fastest.
Arguments:
- ensemble: bfloat16 [1024, 65536], P('narrow', 'wide'), may hold values from -6 to 6
- owner: int32 [512], P('wide'), may hold values from 0 to 63, as said below
- inflation: float32 [64], replicated, may hold values from 1 to 2
- obs_block: int32 [128], P('wide'), may hold values from 0 to 63
- obs_value: float32 [16384], P('wide'), may hold values from -12 to 12
- obs_std: float32 [16384], P('wide'), may hold values from 1 to 300
Outputs:
- analysis: bfloat16 [1024, 65536], P('narrow', 'wide')
Inputs may be any that keep to these rules, and one draw needn't show every extreme that they name: `obs_block`: indexes one of the 64 state blocks held by the same index of wide as the observations. `owner`: a state block held by index w of wide belongs to one of the compartments w * 8 to w * 8 + 7.
All inputs are finite; a program needn't handle non-finite values.
Results may differ from a plain program's by a relative error of at most 0.0069.
Values may be sent and summed in bfloat16 or wider, within the bound.
No kernel may reach another device: no remote copies, remote signals or barrier semaphores. Data moves between devices by JAX's collectives and lax.ppermute only.
A program may use at most 64 MiB of HBM per device.

v0:
```python
import math

import jax
import jax.numpy as jnp
from jax import lax
from jax.sharding import PartitionSpec as P

CLASSES = 128
ITERS = 4


HIGH = lax.Precision.HIGHEST


def row_identity(row_count, members, first_row):
    row_ids = lax.broadcasted_iota(jnp.int32, (row_count, members), 0) + first_row
    col_ids = lax.broadcasted_iota(jnp.int32, (row_count, members), 1)
    return (row_ids == col_ids).astype(jnp.float32)


def on_device(ensemble, owner, inflation, obs_block, obs_value, obs_std):
    local_members, local_states = ensemble.shape
    members = local_members * lax.axis_size("narrow")
    block_count = local_states // CLASSES
    obs_local = obs_value.shape[0]
    scale_root = math.sqrt(members - 1)
    column_sum = jnp.sum(ensemble, axis=0, dtype=jnp.float32)
    state_mean = lax.psum(column_sum, "narrow") / members
    compartments = lax.broadcasted_iota(jnp.int32, (block_count, inflation.shape[0]), 1)
    block_factor = jnp.sum(
        jnp.where(owner[:, None] == compartments, inflation[None, :], 0.0), axis=1
    )
    row_factor = jnp.repeat(block_factor, CLASSES)
    anomaly = (row_factor * (ensemble.astype(jnp.float32) - state_mean)).astype(jnp.bfloat16)
    observed = jnp.take(anomaly.reshape(local_members, block_count, CLASSES), obs_block, axis=1)
    observed = observed.reshape(local_members, obs_local)
    observed_mean = jnp.take(state_mean.reshape(block_count, CLASSES), obs_block, axis=0).reshape(
        obs_local
    )
    scaled = (observed.astype(jnp.float32) / (obs_std * scale_root)).astype(jnp.bfloat16)
    innovation = (obs_value - observed_mean) / obs_std
    spread = lax.all_to_all(scaled, "narrow", split_axis=1, concat_axis=0, tiled=True)
    obs_share = spread.shape[1]
    narrow_index = lax.axis_index("narrow")
    innovation_share = lax.dynamic_slice_in_dim(innovation, narrow_index * obs_share, obs_share)
    projected_part = jnp.dot(spread.astype(jnp.float32), innovation_share, precision=HIGH)
    row_count = members // lax.axis_size("wide")
    first_row = lax.axis_index("wide") * row_count
    identity_rows = row_identity(row_count, members, first_row)
    contract = (((1,), (1,)), ((), ()))
    gram_part = lax.dot_general(spread, spread, contract, preferred_element_type=jnp.float32)
    gram_sum, projected = lax.psum((gram_part, projected_part), ("wide", "narrow"))
    gram_matrix = gram_sum + jnp.eye(members, dtype=jnp.float32)
    frob_norm = jnp.sqrt(jnp.sum(gram_matrix * gram_matrix))
    gram_rows = lax.dynamic_slice_in_dim(gram_matrix, first_row, row_count, 0)
    unit_rows = gram_rows / frob_norm
    iterate = 1.5 * identity_rows - 0.5 * unit_rows
    for turn_index in range(ITERS - 1):
        iterate_all = lax.all_gather(iterate, "wide", axis=0, tiled=True)
        product_one = jnp.dot(unit_rows, iterate_all, precision=HIGH)
        product_two = jnp.dot(product_one, iterate_all, precision=HIGH)
        iterate = 1.5 * iterate - 0.5 * jnp.dot(product_two, iterate_all, precision=HIGH)
    root_rows = iterate / jnp.sqrt(frob_norm)
    midway_rows = jnp.dot(root_rows, projected, precision=HIGH)
    midway = lax.all_gather(midway_rows, "wide", axis=0, tiled=True)
    mean_shift = jnp.dot(root_rows, midway, precision=HIGH) / scale_root
    transform_part = (root_rows + mean_shift[:, None]).astype(jnp.bfloat16)
    transform = lax.all_gather(transform_part, "wide", axis=0, tiled=True)
    state_share = lax.all_to_all(anomaly, "narrow", split_axis=1, concat_axis=0, tiled=True)
    row_share = state_share.shape[1]
    mean_share = lax.dynamic_slice_in_dim(state_mean, narrow_index * row_share, row_share)
    update = lax.dot_general(
        transform, state_share, (((0,), (0,)), ((), ())), preferred_element_type=jnp.float32
    )
    analysis_share = (mean_share[None, :] + update).astype(jnp.bfloat16)
    return lax.all_to_all(analysis_share, "narrow", split_axis=0, concat_axis=1, tiled=True)


def solution(mesh):
    return jax.shard_map(
        on_device,
        mesh=mesh,
        in_specs=(P("narrow", "wide"), P("wide"), P(), P("wide"), P("wide"), P("wide")),
        out_specs=P("narrow", "wide"),
        check_vma=False,
    )
```

profile of v0, /device:TPU:0, one launch (start us, length us, event | category | flops | bytes accessed | tf_op | source)
XLA Modules:
  0.0 614.5 jit_solution(2839341183659462295)
XLA Ops:
  6.5 0.7 compare_and_fusion
  7.2 0.7 compare_select_fusion
  7.9 0.1 broadcast_in_dim.49
  7.9 0.1 broadcast_bitcast_fusion.1
  8.0 0.7 broadcast_multiply_fusion.1
  8.8 0.8 select_reduce_fusion
  9.7 6.4 %copy.21 = bf16[256,8192]{0,1:T(8,128)(2,1)} copy(bf16[256,8192]{1,0:T(8,128)(2,1)} %param.6) | data formatting | bytes 8388608 | tf_op args[0]
  16.1 3.3 convert_reduce_fusion
  19.4 12.9 %psum.21 = f32[8192]{0:T(1024)S(1)} all-reduce(f32[8192]{0:T(1024)S(1)} %convert_reduce_fusion), channel_id=1, replica_groups=mesh['wide'=8,'narrow'=4] {'narrow'}, use_global_device_ids=true, to_apply=%region_1.0 | all-reduce | flops 8192 | bytes 65536 | tf_op jit(solution)/shard_map/psum | solution.py:28
  32.3 5.8 fusion.1
  38.1 6.3 %copy.22 = bf16[256,64,128]{2,0,1:T(8,128)(2,1)} copy(bf16[256,64,128]{0,2,1:T(8,128)(2,1)} %bitcast.67) | data formatting | bytes 8388608 | tf_op jit(solution)/shard_map/reshape | solution.py:35
  44.5 2.9 gather_fusion
  47.4 0.5 copy.23
  48.0 0.7 divide_convert_fusion
  48.7 16.9 %all_to_all.54 = bf16[256,4,512]{0,2,1:T(8,128)(2,1)S(1)} all-to-all(bf16[256,4,512]{0,2,1:T(8,128)(2,1)S(1)} %divide_convert_fusion), channel_id=1, replica_groups=mesh['wide'=8,'narrow'=4] {'narrow'}, dimensions={1} | all-to-all | bytes 2097152 | tf_op jit(solution)/shard_map/all_to_all | solution.py:42
  65.6 0.5 copy.24
  66.1 3.2 fusion.12
  69.4 142.1 %all-reduce.2.cloned.1.call-done = f32[1024,1024]{1,0:T(8,128)} async-done(((f32[1024,1024]{1,0:T(8,128)}), f32[1024,1024]{1,0:T(8,128)}) %all-reduce.2.cloned.1.call-update) | async-done | bytes 4194320 | tf_op jit(solution)/shard_map/psum | solution.py:52
  211.5 5.9 convert_add_fusion
  218.2 2.0 multiply_subtract_fusion
  220.2 0.2 all-gather.8.cloned.1.call-start
  220.5 72.2 %all-gather.6.cloned.1.call-done = f32[1024,1024]{1,0:T(8,128)} async-done(((f32[128,1024]{1,0:T(8,128)}), f32[1024,1024]{1,0:T(8,128)}) %all-gather.6.cloned.1.call-update) | async-done | bytes 4194320 | tf_op jit(solution)/shard_map/all_gather | solution.py:59
  292.7 4.9 fusion.11
  297.6 2.4 fusion.13
  300.0 3.2 fusion.2
  303.3 0.3 all-gather.10.cloned.1.call-start
  303.5 71.5 %all-gather.8.cloned.1.call-done = f32[1024,1024]{1,0:T(8,128)} async-done(((f32[128,1024]{1,0:T(8,128)}), f32[1024,1024]{1,0:T(8,128)}) %all-gather.8.cloned.1.call-update) | async-done | bytes 4194320 | tf_op jit(solution)/shard_map/all_gather | solution.py:59
  375.1 4.9 fusion.10
  380.0 2.4 fusion.14
  382.4 3.2 fusion.3
  385.7 0.6 gather_fusion.1
  386.4 0.8 dynamic-slice_divide_fusion.1
  387.2 0.9 fusion.16
  388.1 39.8 %psum.23 = f32[1024]{0:T(1024)S(1)} all-reduce(f32[1024]{0:T(1024)S(1)} %bitcast.78), channel_id=1, replica_groups=mesh['wide'=8,'narrow'=4] {'wide','narrow'}, use_global_device_ids=true, to_apply=%region_5.6 | all-reduce | flops 1024 | bytes 8192 | tf_op jit(solution)/shard_map/psum | solution.py:52
  427.9 31.0 %all-gather.10.cloned.1.call-done = f32[1024,1024]{1,0:T(8,128)} async-done(((f32[128,1024]{1,0:T(8,128)}), f32[1024,1024]{1,0:T(8,128)}) %all-gather.10.cloned.1.call-update) | async-done | bytes 4194320 | tf_op jit(solution)/shard_map/all_gather | solution.py:59
  458.9 4.9 fusion.9
  463.8 2.4 fusion.15
  466.2 2.4 fusion.5
  468.7 0.5 convolution_bitcast_fusion.1
  469.2 17.7 %all-gather = f32[8,1,128]{2,1,0:T(1,128)S(1)} all-gather(f32[1,1,128]{2,1,0:T(1,128)S(1)} %convolution_bitcast_fusion.1), channel_id=1, replica_groups=mesh['wide'=8,'narrow'=4] {'wide'}, dimensions={0}, use_global_device_ids=true | all-gather | bytes 4608 | tf_op jit(solution)/shard_map/all_gather | solution.py:65
  486.9 0.5 fusion.6
  487.5 0.8 add_convert_fusion.1
  488.3 5.1 all-to-all-start.1
  493.4 47.9 %all-to-all-done.1 = bf16[256,4,2048]{0,2,1:T(8,128)(2,1)} async-done(((bf16[256,4,2048]{0,2,1:T(8,128)(2,1)}), bf16[256,4,2048]{0,2,1:T(8,128)(2,1)}, u32[]{:S(2)}, u32[]{:S(2)}) %all-to-all-start.1) | async-done | bytes 4194336 | tf_op jit(solution)/shard_map/all_to_all | solution.py:69
  541.4 6.2 %copy.25 = bf16[4,256,2048]{2,1,0:T(8,128)(2,1)} copy(bf16[4,256,2048]{1,2,0:T(8,128)(2,1)} %bitcast.17) | data formatting | bytes 8388608 | tf_op jit(solution)/shard_map/all_to_all | solution.py:69
  547.5 7.4 %add_convert_fusion = bf16[1024,2048]{1,0:T(8,128)(2,1)S(1)} fusion(f32[2048]{0:T(1024)S(1)} %dynamic_slice.9, bf16[1024,1024]{1,0:T(8,128)(2,1)} %all-gather.12.cloned.1.call-done, bf16[1024,2048]{1,0:T(8,128)(2,1)} %bitcast.72), kind=kOutput, calls=%fused_computation.6 | convolution fusion | flops 4299161600 | bytes 10493952 | tf_op jit(solution)/shard_map/dot_general | solution.py:72
  555.0 50.7 %all_to_all.55 = bf16[4,256,2048]{2,1,0:T(8,128)(2,1)S(1)} all-to-all(bf16[4,256,2048]{2,1,0:T(8,128)(2,1)S(1)} %bitcast.73), channel_id=1, replica_groups=mesh['wide'=8,'narrow'=4] {'narrow'}, dimensions={0} | all-to-all | bytes 8388608 | tf_op jit(solution)/shard_map/all_to_all | solution.py:76
  605.7 2.3 copy.27
  (29 shorter events, 0.4 us)
Async XLA Ops:
  6.5 205.0 %all-reduce.2.cloned.1.call-start = ((), (), s32[]{:S(2)}) async-start(), calls=%async_computation.3 | async-start | bytes 8388608 | tf_op jit(solution)/shard_map/psum | solution.py:52
  69.4 223.3 %all-gather.6.cloned.1.call-start = ((), (), s32[]{:S(2)}) async-start(), calls=%async_computation.4 | async-start | bytes 4718592 | tf_op jit(solution)/shard_map/all_gather | solution.py:59
  220.2 79.8 %copy-start.4 = (f32[128,1024]{1,0:T(8,128)S(1)}, f32[128,1024]{1,0:T(8,128)}, u32[]{:S(2)}) copy-start(f32[128,1024]{1,0:T(8,128)} %multiply_subtract_fusion) | copy-start | bytes 1572868
  220.2 154.9 %all-gather.8.cloned.1.call-start = ((), (), s32[]{:S(2)}) async-start(), calls=%async_computation.5 | async-start | bytes 4718592 | tf_op jit(solution)/shard_map/all_gather | solution.py:59
  292.7 4.9 copy-start.1
  303.3 79.1 %copy-start.5 = (f32[128,1024]{1,0:T(8,128)S(1)}, f32[128,1024]{1,0:T(8,128)}, u32[]{:S(2)}) copy-start(f32[128,1024]{1,0:T(8,128)} %fusion.2) | copy-start | bytes 1572868
  303.3 155.6 %all-gather.10.cloned.1.call-start = ((), (), s32[]{:S(2)}) async-start(), calls=%async_computation.6 | async-start | bytes 4718592 | tf_op jit(solution)/shard_map/all_gather | solution.py:59
  375.1 4.9 copy-start.2
  385.7 161.9 %all-gather.12.cloned.1.call-start = ((), (), s32[]{:S(2)}) async-start(), calls=%async_computation.7 | async-start | bytes 2359296 | tf_op jit(solution)/shard_map/all_gather | solution.py:68
  427.9 38.3 %copy-start.3 = (f32[128,1024]{1,0:T(8,128)S(1)}, f32[128,1024]{1,0:T(8,128)}, u32[]{:S(2)}) copy-start(f32[128,1024]{1,0:T(8,128)} %fusion.3) | copy-start | bytes 1572868
  458.9 4.9 copy-start
  488.3 53.1 %all-to-all-start.1 = ((bf16[256,4,2048]{0,2,1:T(8,128)(2,1)}), bf16[256,4,2048]{0,2,1:T(8,128)(2,1)}, u32[]{:S(2)}, u32[]{:S(2)}) async-start(bf16[256,4,2048]{0,2,1:T(8,128)(2,1)} %bitcast.68), calls=%async_computation.1 | async-start | bytes 8388608 | tf_op jit(solution)/shard_map/all_to_all | solution.py:69
Sparse Core Ops, SparseCore 0:
  69.5 142.0 all-reduce.1
  220.3 72.2 all-gather.5
  303.4 71.6 all-gather.7
  385.8 73.0 all-gather.9
  488.4 46.4 all-gather.11
where the time goes:
time: 616 us; the launch traced here: 615 us
  waiting for transfers between devices  365 us (59%)
  blocking collectives  138 us (22%)
  matrix products  43.4 us (7%)
  local copies, waits for them, and re-layouts  26.1 us (4%)
  other arithmetic  22.3 us (4%)
  between operations  14.2 us (2%)
    all_gather x3, waiting for transfers between devices, on_device(): iterate_all = lax.all_gather(iterate, 'wide', axis=0, tiled=True)  175 us
    psum x1, waiting for transfers between devices, on_device(): lax.psum((gram_part, projected_part), ('wide', 'narrow'))  142 us
    all_to_all x1, blocking collectives, on_device(): lax.all_to_all(analysis_share, 'narrow', split_axis=0, concat_axis=1, til...  50.7 us
    all_to_all x1, waiting for transfers between devices, on_device(): lax.all_to_all(anomaly, 'narrow', split_axis=1, concat_axis=0, tiled=True)  47.9 us
    psum x1, blocking collectives, on_device(): lax.psum((gram_part, projected_part), ('wide', 'narrow'))  39.8 us
    all_gather x1, blocking collectives, on_device(): midway = lax.all_gather(midway_rows, 'wide', axis=0, tiled=True)  17.7 us
    all_to_all x1, blocking collectives, on_device(): lax.all_to_all(scaled, 'narrow', split_axis=1, concat_axis=0, tiled=True)  16.9 us
    dot_general x3, matrix products, on_device(): product_one = jnp.dot(unit_rows, iterate_all, precision=HIGH)  14.7 us
  transfers between devices with their start and end apart: 6, of which 5 were waited for; matrix products, arithmetic and copies ran while one was open for 1% of the time, Pallas kernels for 0%

commit v1 on v0

v1 whole, which is shorter than its diff:
```python
import functools
import math

import jax
import jax.numpy as jnp
from jax import lax
from jax.experimental import pallas as pl
from jax.experimental.pallas import tpu as pltpu
from jax.sharding import PartitionSpec as P

CLASSES = 128
PAD = 16
LANES = 128
F32 = jnp.float32
BF16 = jnp.bfloat16
ANY = pl.BlockSpec(memory_space=pl.ANY)
HBM = pl.BlockSpec(memory_space=pltpu.HBM)
SMEM = pl.BlockSpec(memory_space=pltpu.SMEM)
VMEM = pl.BlockSpec(memory_space=pltpu.VMEM)
MIB = 1024 * 1024


def dot(a, b):
    return lax.dot_general(a, b, (((1,), (0,)), ((), ())), preferred_element_type=F32)


def dot_nt(a, b):
    return lax.dot_general(a, b, (((1,), (1,)), ((), ())), preferred_element_type=F32)


def swap(x, axis, mask):
    size = lax.axis_size(axis)
    return lax.ppermute(x, axis, [(i, i ^ mask) for i in range(size)])


def masks_of(size):
    return [1 << b for b in range(size.bit_length() - 1)]


def far(x):
    held = {0: x}
    for mask in reversed(masks_of(lax.axis_size("narrow"))[1:]):
        for m in list(held):
            held[m ^ mask] = swap(held[m], "narrow", mask)
    return held


def near(held, own=None):
    both = dict(held)
    for m in held:
        both[m ^ 1] = swap(held[m], "narrow", 1) if m or own is None else own
    return [both[m] for m in range(len(both))]


def tie(*trees):
    return lax.optimization_barrier(trees)


def lead_kernel(obs_ref, ens_ref, order_ref, lead_ref, mark_ref, sem):
    nob = obs_ref.shape[0]
    nblk = mark_ref.shape[0]

    for i in range(nblk):
        mark_ref[i] = 0
    place = 0
    for i in range(nob):
        block = obs_ref[i]
        order_ref[place] = block
        place = place + 1 - mark_ref[block]
        mark_ref[block] = 1
    for i in range(nblk):
        order_ref[place] = i
        place = place + 1 - mark_ref[i]
    copy_blocks(order_ref, 0, ens_ref, lead_ref, sem)
    wait_blocks(ens_ref, lead_ref, sem)


def copy_blocks(order_ref, first, ens_ref, out_ref, sem):
    count = out_ref.shape[1] // CLASSES

    def start(q, c):
        src = pl.multiple_of(order_ref[first + q] * CLASSES, CLASSES)
        dst = pl.multiple_of(q * CLASSES, CLASSES)
        pltpu.make_async_copy(
            ens_ref.at[:, pl.ds(src, CLASSES)], out_ref.at[:, pl.ds(dst, CLASSES)], sem
        ).start()
        return c

    lax.fori_loop(0, count, start, 0, unroll=4)


def wait_blocks(ens_ref, out_ref, sem):
    pltpu.make_async_copy(ens_ref.at[:, pl.ds(0, out_ref.shape[1])], out_ref, sem).wait()


def lead_blocks(obs_block, ensemble, lead):
    members, states = ensemble.shape
    nblk = states // CLASSES
    return pl.pallas_call(
        lead_kernel,
        out_shape=(
            jax.ShapeDtypeStruct((2 * nblk,), jnp.int32),
            jax.ShapeDtypeStruct((members, lead * CLASSES), BF16),
        ),
        in_specs=[SMEM, HBM],
        out_specs=(SMEM, VMEM),
        scratch_shapes=[pltpu.SMEM((nblk,), jnp.int32), pltpu.SemaphoreType.DMA],
        compiler_params=pltpu.CompilerParams(vmem_limit_bytes=60 * MIB),
        name="lead_blocks",
    )(obs_block, ensemble)


def rest_kernel(lead, order_ref, ens_ref, *refs):
    outs, sems = refs[:-1], refs[-1]
    first = lead
    for c, out in enumerate(outs):
        copy_blocks(order_ref, first, ens_ref, out, sems.at[c])
        first += out.shape[1] // CLASSES
    for c, out in enumerate(outs):
        wait_blocks(ens_ref, out, sems.at[c])


def rest_blocks(order, ensemble, lead, sizes):
    members = ensemble.shape[0]
    count = len(sizes)
    return pl.pallas_call(
        functools.partial(rest_kernel, lead),
        out_shape=[jax.ShapeDtypeStruct((members, n * CLASSES), BF16) for n in sizes],
        in_specs=[SMEM, HBM],
        out_specs=[VMEM] * count,
        scratch_shapes=[pltpu.SemaphoreType.DMA((count,))],
        compiler_params=pltpu.CompilerParams(vmem_limit_bytes=56 * MIB),
        name="rest_blocks",
    )(order, ensemble)


def split_rows(row, count, terms):
    ids = lax.broadcasted_iota(jnp.int32, (count, row.shape[1]), 0)
    out = jnp.zeros((count, row.shape[1]), F32)
    left = row
    for t in range(terms):
        part = left.astype(BF16).astype(F32)
        out = jnp.where(ids == t, part, out)
        left = left - part
    return out.astype(BF16)


def tail_of(rows, count):
    high = rows.astype(BF16).astype(F32)
    below = jnp.zeros((count - 2 * rows.shape[0], rows.shape[1]), F32)
    return jnp.concatenate([high, rows - high, below], axis=0).astype(BF16)


def rows_of_tail(tail):
    tail = tail.astype(F32)
    return tail[:8] + tail[8:16]


def slab_width(own, local):
    pairs = own * (own - 1) // 2 + own * own // 2
    return own * 3 // 2 * (local // 2) + pairs * local


def is_high(index_ref):
    return lax.rem(index_ref[0], 2) == 1


def gram_kernel(parts, scale_root, width, *refs):
    index_ref = refs[0]
    raws = refs[1 : parts + 1]
    factor_ref, weight_ref, root_ref, level_ref = refs[parts + 1 : parts + 5]
    keep_one, send_one, keep_two, send_two, halves, scaled, own, pulls = refs[parts + 5 :]
    local, cols = raws[0].shape
    half = local // 2
    count = parts // 2
    for first in range(0, cols, width):
        part = slice(first, first + width)
        factor = factor_ref[:, part]
        values = [r[:, part].astype(F32) for r in raws]
        total = jnp.sum(values[0], axis=0, keepdims=True)
        for v in values[1:]:
            total = total + jnp.sum(v, axis=0, keepdims=True)
        mean = total / (local * parts)
        both = factor * root_ref[:, part]
        for m, v in enumerate(values):
            v = v - mean
            place = (m % 2 * count + m // 2) * local
            scaled[place : place + local, part] = (both * v).astype(BF16)
            if m % 2 == 0:
                own[m // 2 * local : (m // 2 + 1) * local, part] = (factor * v).astype(BF16)
        pull = level_ref[:, part] - mean * weight_ref[:, part] * scale_root
        pulls[:, part] = split_rows(pull, PAD, 3)

    high = is_high(index_ref)
    at = [0, 0]

    def put(which, value):
        halves[which, :, at[which] : at[which] + value.shape[1]] = value.astype(BF16)
        at[which] += value.shape[1]

    side = count * local
    blocks = {}
    for j in range(count):
        product = dot_nt(scaled[j * local : side, :], scaled[j * local : (j + 1) * local, :])
        for i in range(j, count):
            blocks[i, j] = product[(i - j) * local : (i - j + 1) * local]
    for i in range(count):
        put(i % 2, blocks[i, i][:half, :half])
        put(1 - i % 2, blocks[i, i][half:, :])
    for i in range(count):
        for j in range(i):
            put(0, blocks[i, j][:half])
            put(1, blocks[i, j][half:])
    low = scaled[pl.ds(pl.multiple_of(jnp.where(high, side, 0), side), side), :]
    for c in range(count // 2):
        first = jnp.where(high, (c + count // 2) * local, side + c * local)
        product = dot_nt(low, scaled[pl.ds(pl.multiple_of(first, local), local), :])
        for i in range(count):
            blocks[i, c] = product[i * local : (i + 1) * local]
    for i in range(count):
        for c in range(count // 2):
            put(0, blocks[i, c][:half])
            put(1, blocks[i, c][half:])
    row = jnp.sum(dot_nt(pulls[...], own[...]), axis=0, keepdims=True)
    ids = lax.broadcasted_iota(jnp.int32, (8, LANES), 0)
    rows = jnp.zeros((8, LANES), F32)
    for r in range(side // LANES):
        rows = jnp.where(ids == r, row[:, r * LANES : (r + 1) * LANES], rows)
    quarter = half // 2
    across = halves.shape[2]
    mine = pl.multiple_of(index_ref[1] * quarter, quarter)
    other = pl.multiple_of((1 - index_ref[1]) * quarter, quarter)
    for ref, which, first in (
        (keep_one, 0, mine),
        (send_one, 0, other),
        (keep_two, 1, mine),
        (send_two, 1, other),
    ):
        ref[:, :across] = halves[which, pl.ds(first, quarter), :]
        if which == 0:
            ref[:, across:] = tail_of(rows, quarter)


def gram_rows(index, raws, factor, weight, root, level, scale_root, width=256):
    parts = len(raws)
    local, cols = raws[0].shape
    half = local // 2
    members = local * parts
    across = slab_width(parts // 2, local)
    return pl.pallas_call(
        functools.partial(gram_kernel, parts, scale_root, width),
        out_shape=(
            jax.ShapeDtypeStruct((half // 2, across + LANES), BF16),
            jax.ShapeDtypeStruct((half // 2, across + LANES), BF16),
            jax.ShapeDtypeStruct((half // 2, across), BF16),
            jax.ShapeDtypeStruct((half // 2, across), BF16),
        ),
        in_specs=[SMEM] + [VMEM] * (parts + 4),
        out_specs=(VMEM, VMEM, VMEM, VMEM),
        scratch_shapes=[
            pltpu.VMEM((2, half, across), BF16),
            pltpu.VMEM((members, cols), BF16),
            pltpu.VMEM((members // 2, cols), BF16),
            pltpu.VMEM((PAD, cols), BF16),
        ],
        compiler_params=pltpu.CompilerParams(vmem_limit_bytes=24 * MIB),
        cost_estimate=pl.CostEstimate(flops=1024, bytes_accessed=1024, transcendentals=0),
        name="gram_rows",
    )(index, *raws, factor, weight, root, level)


def add_kernel(across, a_ref, b_ref, out_ref):
    both = a_ref[:, :across].astype(F32) + b_ref[:, :across].astype(F32)
    out_ref[:, :across] = both.astype(BF16)
    if across < a_ref.shape[1]:
        rows = rows_of_tail(a_ref[:, across:]) + rows_of_tail(b_ref[:, across:])
        out_ref[:, across:] = tail_of(rows, a_ref.shape[0])


def add_slabs(a, b, across):
    return pl.pallas_call(
        functools.partial(add_kernel, across),
        out_shape=jax.ShapeDtypeStruct(a.shape, BF16),
        in_specs=[VMEM, VMEM],
        out_specs=VMEM,
        compiler_params=pltpu.CompilerParams(vmem_limit_bytes=16 * MIB),
        name="add_slabs",
    )(a, b)


def join_kernel(index_ref, one_ref, other_one_ref, two_ref, other_two_ref, out_ref):
    quarter, across = two_ref.shape
    mine = pl.multiple_of(index_ref[1] * quarter, quarter)
    other = pl.multiple_of((1 - index_ref[1]) * quarter, quarter)
    out_ref[pl.ds(mine, quarter), :across] = one_ref[:, :across]
    out_ref[pl.ds(other, quarter), :across] = other_one_ref[:, :across]
    out_ref[pl.ds(2 * quarter + mine, quarter), :across] = two_ref[...]
    out_ref[pl.ds(2 * quarter + other, quarter), :across] = other_two_ref[...]
    out_ref[:quarter, across:] = one_ref[:, across:]
    out_ref[quarter:, across:] = jnp.zeros((3 * quarter, out_ref.shape[1] - across), BF16)


def join_slabs(index, one, other_one, two, other_two):
    quarter = two.shape[0]
    return pl.pallas_call(
        join_kernel,
        out_shape=jax.ShapeDtypeStruct((4 * quarter, one.shape[1]), BF16),
        in_specs=[SMEM] + [VMEM] * 4,
        out_specs=VMEM,
        compiler_params=pltpu.CompilerParams(vmem_limit_bytes=16 * MIB),
        name="join_slabs",
    )(index, one, other_one, two, other_two)


def root_kernel(parts, scale_root, tile, *refs):
    index_ref, mine_ref, sibling_ref, out_ref = refs[:4]
    u, ub, rest, rb, work, wb, wb2, tail = refs[4:]
    members = u.shape[0]
    local = members // parts
    half = local // 2
    count = parts // 2
    diag = lax.broadcasted_iota(jnp.int32, (local, local), 0) == lax.broadcasted_iota(
        jnp.int32, (local, local), 1
    )
    square = jnp.zeros((1, members), F32)

    def span(m):
        return slice(m * local, (m + 1) * local)

    def put_pair(i, j, block):
        u[span(i), span(j)] = block
        u[span(j), span(i)] = block.T

    high = is_high(index_ref)
    crossed = []
    for side, slab in enumerate((mine_ref, sibling_ref)):
        at = [0, 0]

        def take(which, width):
            first = at[which]
            at[which] += width
            return slab[which * half : (which + 1) * half, first : first + width].astype(F32)

        for i in range(count):
            corner = take(i % 2, half)
            lower = take(1 - i % 2, local)
            upper = jnp.concatenate([corner, lower[:, :half].T], axis=1)
            block = jnp.concatenate([upper, lower], axis=0) + jnp.where(diag, 1.0, 0.0)
            u[span(2 * i + side), span(2 * i + side)] = block
        for i in range(count):
            for j in range(i):
                block = jnp.concatenate([take(0, local), take(1, local)], axis=0)
                put_pair(2 * i + side, 2 * j + side, block)
        for i in range(count):
            for c in range(count // 2):
                block = jnp.concatenate([take(0, local), take(1, local)], axis=0)
                crossed.append((side, i, c, block))
    for side, i, c, block in crossed:

        @pl.when(high)
        def _():
            put_pair(2 * i + 1, 2 * (c + (1 - side) * (count // 2)), block)

        @pl.when(jnp.logical_not(high))
        def _():
            put_pair(2 * i, 2 * (c + side * (count // 2)) + 1, block)

    for m in range(parts):
        part = u[m * local : (m + 1) * local, :]
        square = square + jnp.sum(part * part, axis=0, keepdims=True)
    frob = jnp.sqrt(jnp.sum(square, axis=1, keepdims=True))

    def each_column(body):
        for first in range(0, members, tile):
            body(slice(first, members), slice(first, first + tile))

    def mirror(ref, below, col, value):
        value = value.astype(BF16)
        ref[below, col] = value
        for first in range(col.stop, members, tile):
            block = value[first - col.start : first - col.start + tile]
            ref[col, first : first + tile] = block.T

    inverse = 1.0 / frob
    unit = u[...] * inverse
    u[...] = unit
    ub[:members, :] = unit.astype(BF16)

    def square_columns(below, col):
        v = dot(ub[below, :], ub[:members, col])
        unit = u[below, col]
        mirror(wb, below, col, v)
        mirror(wb2, below, col, 0.0625 * v - 0.5625 * unit)
        rest[below, col] = 1.6875 * v - 2.4375 * unit

    def second_columns(below, col):
        r = rest[below, col] + dot(wb[below, :], wb2[:, col])
        rest[below, col] = r
        mirror(rb, below, col, r)

    each_column(square_columns)
    each_column(second_columns)

    sums = []
    for slab in (mine_ref, sibling_ref):
        rows = rows_of_tail(slab[:PAD, slab.shape[1] - LANES :])
        pieces = [rows[r : r + 1, :] for r in range(count * local // LANES)]
        sums.append(jnp.concatenate(pieces, axis=1))
    projected = jnp.concatenate(
        [sums[m % 2][:, m // 2 * local : (m // 2 + 1) * local] for m in range(parts)], axis=1
    )
    ub[members:, :] = split_rows(projected, PAD, 2)

    def z_columns(below, col):
        y = dot(ub[below.start :, :], rb[:members, col])
        z = 2.25 * u[below, col] + y[:-PAD]
        tail[:, col] = y[-PAD:]
        work[below, col] = z
        mirror(wb, below, col, z)

    def a_columns(below, col):
        a = 2.25 * work[below, col] + dot(wb[below, :], rb[:members, col])
        mirror(wb2, below, col, a)
        rest[below, col] = 1.5 * rest[below, col] - 1.125 * a

    def third_columns(below, col):
        y = dot(rb[below.start :, :], wb2[:, col])
        r = rest[below, col] - 0.5 * y[:-PAD]
        tail[:, col] = y[-PAD:]
        rest[below, col] = r
        mirror(wb, below, col, r)

    each_column(z_columns)
    second_row = 2.25 * projected + jnp.sum(tail[...], axis=0, keepdims=True)
    rb[members:, :] = split_rows(second_row, PAD, 2)
    each_column(a_columns)
    each_column(third_columns)
    third_row = 1.5 * second_row - 0.5 * jnp.sum(tail[...], axis=0, keepdims=True)
    rest_rows = rest[:, :local].T

    def times(slab, row, mat):
        y = dot(jnp.concatenate([slab.astype(BF16), split_rows(row, PAD, 2)], axis=0), mat)
        return y[:local], jnp.sum(y[local:], axis=0, keepdims=True)

    def row_times(row, mat):
        return jnp.sum(dot(split_rows(row, PAD, 2), mat), axis=0, keepdims=True)

    unit_cols = ub[:members, :]
    rest_cols = wb[...]
    y, z_row = times(rest_rows, third_row, unit_cols)
    z = 3.375 * u[:local, :] + y
    y, a_row = times(z, z_row, rest_cols)
    a, a_row = 3.375 * z + y, 3.375 * z_row + a_row
    y, b_row = times(a, a_row, rest_cols)
    b, b_row = 3.375 * a + y, 3.375 * a_row + b_row
    eye = jnp.concatenate(
        [jnp.where(diag, 3.375, 0.0), jnp.zeros((local, members - local), F32)], axis=1
    )
    fourth = 1.5 * (eye + rest_rows) - 0.5 * b
    midway = 1.5 * third_row - 0.5 * b_row
    y_row = 3.375 * midway + row_times(midway, rest_cols)
    z_row = row_times(y_row, unit_cols)
    a_row = 3.375 * z_row + row_times(z_row, rest_cols)
    b_row = 3.375 * a_row + row_times(a_row, rest_cols)
    shift = (1.5 * y_row - 0.5 * b_row) * (inverse / scale_root)
    out_ref[...] = (fourth * jnp.sqrt(inverse) + shift).astype(BF16)


def transform_rows(index, mine, sibling, parts, scale_root, tile=256):
    local = mine.shape[0]
    members = local * parts
    wide = pltpu.VMEM((members, members), F32)
    narrow = pltpu.VMEM((members, members), BF16)
    longer = pltpu.VMEM((members + PAD, members), BF16)
    return pl.pallas_call(
        functools.partial(root_kernel, parts, scale_root, tile),
        out_shape=jax.ShapeDtypeStruct((local, members), BF16),
        in_specs=[SMEM] + [VMEM] * 2,
        out_specs=VMEM,
        scratch_shapes=[wide, longer, wide, longer, wide, narrow, narrow]
        + [pltpu.VMEM((PAD, members), F32)],
        compiler_params=pltpu.CompilerParams(vmem_limit_bytes=36 * MIB),
        cost_estimate=pl.CostEstimate(flops=1024, bytes_accessed=1024, transcendentals=0),
        name="transform_rows",
    )(index, mine, sibling)


def sums_kernel(width, *refs):
    out_ref = refs[-1]
    for first in range(0, out_ref.shape[1], width):
        part = slice(first, min(first + width, out_ref.shape[1]))
        out_ref[:, part] = column_sums([r[:, part] for r in refs[:-1]])


def column_sums(pieces):
    total = jnp.sum(pieces[0].astype(F32), axis=0, keepdims=True)
    for piece in pieces[1:]:
        total = total + jnp.sum(piece.astype(F32), axis=0, keepdims=True)
    return total


def sums(pieces, width=256):
    return pl.pallas_call(
        functools.partial(sums_kernel, width),
        out_shape=jax.ShapeDtypeStruct((1, pieces[0].shape[1]), F32),
        in_specs=[VMEM] * len(pieces),
        out_specs=VMEM,
        compiler_params=pltpu.CompilerParams(vmem_limit_bytes=16 * MIB),
        cost_estimate=pl.CostEstimate(flops=1024, bytes_accessed=1024, transcendentals=0),
        name="sums",
    )(*pieces)


def update_kernel(width, parts, start, summed, order_ref, t_ref, factor_ref, *refs):
    raws, totals = refs[: parts * len(summed)], refs[parts * len(summed) : (parts + 1) * len(summed)]
    out_ref, buf, sem = refs[-3:]
    local, members = t_ref.shape
    rows = jnp.sum(t_ref[...].astype(F32), axis=1, keepdims=True)
    col = 0
    for chunk, (done, total_ref) in enumerate(zip(summed, totals)):
        held = raws[chunk * parts : (chunk + 1) * parts]
        for first in range(0, held[0].shape[1], width):
            count = min(width, held[0].shape[1] - first)
            part = slice(first, first + count)
            pieces = [r[:, part] for r in held]
            total = total_ref[:, part]
            if done < parts:
                total = total + column_sums(pieces[done:])
            mean = total / members
            factor = factor_ref[:, start + col : start + col + count]
            product = dot(t_ref[...], jnp.concatenate(pieces, axis=0))
            buf[:, col : col + count] = (
                factor * product + (mean - (mean * factor) * rows)
            ).astype(BF16)
            for q in range(0, count, CLASSES):
                src = col + q
                dst = pl.multiple_of(order_ref[(start + src) // CLASSES] * CLASSES, CLASSES)
                pltpu.make_async_copy(
                    buf.at[:, pl.ds(src, CLASSES)], out_ref.at[:, pl.ds(dst, CLASSES)], sem
                ).start()
            col += count
    pltpu.make_async_copy(buf, out_ref.at[:, pl.ds(0, col)], sem).wait()


def update(order, transform, factor, chunks, totals, summed, start, result=None, width=512):
    local, members = transform.shape
    parts = len(chunks[0])
    states = factor.shape[1]
    cols = sum(raws[0].shape[1] for raws in chunks)
    raws = [x for held in chunks for x in held]
    extra = [] if result is None else [result]
    inputs = raws + totals
    return pl.pallas_call(
        functools.partial(update_kernel, width, parts, start, summed),
        out_shape=jax.ShapeDtypeStruct((local, states), BF16),
        in_specs=[SMEM, VMEM, VMEM] + [VMEM] * len(inputs) + [ANY] * len(extra),
        out_specs=ANY,
        scratch_shapes=[pltpu.VMEM((local, cols), BF16), pltpu.SemaphoreType.DMA],
        input_output_aliases={3 + len(inputs): 0} if extra else {},
        compiler_params=pltpu.CompilerParams(vmem_limit_bytes=24 * MIB),
        cost_estimate=pl.CostEstimate(flops=1024, bytes_accessed=1024, transcendentals=0),
        name="update",
    )(order, transform, factor, *inputs, *extra)


def on_device(ensemble, owner, inflation, obs_block, obs_value, obs_std):
    local, states = ensemble.shape
    parts = lax.axis_size("narrow")
    members = local * parts
    nblk = states // CLASSES
    nob = obs_block.shape[0]
    scale_root = math.sqrt(members - 1)

    order, lead = lead_blocks(obs_block, ensemble, nob)
    lead_far = far(lead)
    left = nblk - nob
    sizes = [left * 30 // 48]
    sizes.append(left - sum(sizes))
    starts = [nob * CLASSES]
    for n in sizes[:-1]:
        starts.append(starts[-1] + n * CLASSES)
    rest = list(rest_blocks(order, ensemble, nob, sizes))

    pick = order[:nblk, None] == jnp.arange(nblk, dtype=jnp.int32)[None, :]
    owner_new = jnp.sum(jnp.where(pick, owner[None, :], 0), axis=1)
    comps = jnp.arange(inflation.shape[0], dtype=jnp.int32)
    factor_new = jnp.sum(
        jnp.where(owner_new[:, None] == comps[None, :], inflation[None, :], 0.0), axis=1
    )
    factor = jnp.repeat(factor_new, CLASSES).reshape(1, states)
    match = (order[:nob, None] == obs_block[None, :])[:, :, None]
    inverse = 1.0 / (obs_std * obs_std)
    weight = jnp.sum(jnp.where(match, inverse.reshape(1, nob, CLASSES), 0.0), axis=1)
    weight = weight.reshape(1, nob * CLASSES) / (members - 1)
    level = jnp.sum(jnp.where(match, (obs_value * inverse).reshape(1, nob, CLASSES), 0.0), axis=1)
    level = level.reshape(1, nob * CLASSES) / scale_root

    root = jnp.sqrt(weight)
    index = jnp.stack([lax.axis_index("narrow"), lax.rem(lax.axis_index("wide"), 2)])
    fars = [far(chunk) for chunk in rest]
    owns = [swap(chunk, "narrow", 1) for chunk in rest]
    lead_far, lead_own, rest, factor, weight, root, level = tie(
        lead_far, swap(lead, "narrow", 1), rest, factor, weight, root, level
    )
    lead_all = near(lead_far, lead_own)
    one, send_one, two, send_two = gram_rows(
        index, lead_all, factor, weight, root, level, scale_root
    )

    across = two.shape[1]
    masks = masks_of(lax.axis_size("wide"))
    steps = masks + [1]
    for slot in range(len(steps) + 1):
        one, two, send_one, send_two = tie(one, two, send_one, send_two)
        got = []
        if slot < len(steps):
            got.append(swap(send_one if slot == 0 else one, "wide", steps[slot]))
        if slot > 0:
            got.append(swap(send_two if slot == 1 else two, "wide", steps[slot - 1]))
        if slot == 0:
            total = sums(lead_all)
            got, total = tie(got, total)
        elif slot == 1:
            early = [sums([chunk, own]) for chunk, own in zip(rest, owns)]
            got, early, owns = tie(got, early, owns)
        elif slot == len(steps) - 1:
            got, fars[0] = tie(got, fars[0])
        else:
            (got,) = tie(got)
        if slot < len(masks):
            one = add_slabs(one, got[0], across)
        elif slot == len(masks):
            other_one = got[0]
        if 0 < slot <= len(masks):
            two = add_slabs(two, got[-1], across)
        elif slot > len(masks):
            other_two = got[-1]
    slab = join_slabs(index, one, other_one, two, other_two)
    sibling, all_one = tie(swap(slab, "narrow", 1), near(fars[0], owns[0]))
    transform = transform_rows(index, slab, sibling, parts, scale_root)
    result = update(order, transform, factor, [all_one], [early[0]], [2], starts[0])
    fars[1], result = tie(fars[1], result)
    all_two = near(fars[1], owns[1])
    result = update(order, transform, factor, [lead_all], [total], [parts], 0, result)
    return update(order, transform, factor, [all_two], [early[1]], [2], starts[1], result)


def solution(mesh):
    return jax.shard_map(
        on_device,
        mesh=mesh,
        in_specs=(P("narrow", "wide"), P("wide"), P(), P("wide"), P("wide"), P("wide")),
        out_specs=P("narrow", "wide"),
        check_vma=False,
    )
```

time: 616 us -> 108 us (0.18)
  waiting for transfers between devices: 365 us -> 45.5 us
  blocking collectives: 138 us -> 0 us
  Pallas kernels: 0 us -> 43.7 us
  matrix products: 43.4 us -> 0 us
  local copies, waits for them, and re-layouts: 26.1 us -> 0.14 us
  other arithmetic: 22.3 us -> 0.64 us
  between operations: 14.2 us -> 0.44 us
  starting transfers between devices: 5.72 us -> 17.3 us
    all_gather x4 -> x0, waiting for transfers between devices: 175 us -> none  [the longest x3 175 us: on_device(): iterate_all = lax.all_gather(iterate, 'wide', axis=0, tiled=True)]
    psum x1 -> x0, waiting for transfers between devices: 142 us -> none  [on_device(): lax.psum((gram_part, projected_part), ('wide', 'narrow'))]
    all_to_all x2 -> x0, blocking collectives: 67.6 us -> none  [the longest x1 50.7 us: on_device(): lax.all_to_all(analysis_share, 'narrow', split_axis=0, concat_axis=1, til...]
    psum x2 -> x0, blocking collectives: 52.7 us -> none  [the longest x1 39.8 us: on_device(): lax.psum((gram_part, projected_part), ('wide', 'narrow'))]
    all_to_all x1 -> x0, waiting for transfers between devices: 47.9 us -> none  [on_device(): lax.all_to_all(anomaly, 'narrow', split_axis=1, concat_axis=0, tiled=True)]
    ppermute x0 -> x18, waiting for transfers between devices: none -> 45.5 us  [swap(): return lax.ppermute(x, axis, [(i, i ^ mask) for i in range(size)])]
    pallas_call x0 -> x17, Pallas kernels: none -> 43.7 us  [the longest x1 12.6 us: transform_rows(): pl.pallas_call(functools.partial(root_kernel, parts, scale_root, tile), o...]
    dot_general x14 -> x0, matrix products: 43.4 us -> none  [the longest x3 14.7 us: on_device(): product_one = jnp.dot(unit_rows, iterate_all, precision=HIGH)]
  transfers between devices with their start and end apart: 6 -> 18, of which waited for: 5 -> 7; matrix products, arithmetic and copies ran while one was open for 1% -> 1% of each run, Pallas kernels for 0% -> 34%
where the time goes in v1:
time: 108 us
  waiting for transfers between devices  45.5 us (42%)
  Pallas kernels  43.7 us (40%)
  starting transfers between devices  17.3 us (16%)
    ppermute x18, waiting for transfers between devices, swap(): return lax.ppermute(x, axis, [(i, i ^ mask) for i in range(size)])  45.5 us
    ppermute x18, starting transfers between devices, swap(): return lax.ppermute(x, axis, [(i, i ^ mask) for i in range(size)])  17.3 us
    pallas_call x1, Pallas kernels, transform_rows(): pl.pallas_call(functools.partial(root_kernel, parts, scale_root, tile), o...  12.6 us
    pallas_call x3, Pallas kernels, update(): pl.pallas_call(functools.partial(update_kernel, width, parts, start, summ...  12.4 us
    pallas_call x3, Pallas kernels, sums(): pl.pallas_call(functools.partial(sums_kernel, width), out_shape=jax.Shape...  5.62 us
    pallas_call x1, Pallas kernels, gram_rows(): pl.pallas_call(functools.partial(gram_kernel, parts, scale_root, width),...  4.67 us
    pallas_call x1, Pallas kernels, rest_blocks(): pl.pallas_call(functools.partial(rest_kernel, lead), out_shape=[jax.Shape...  4.48 us
    pallas_call x1, Pallas kernels, lead_blocks(): pl.pallas_call(lead_kernel, out_shape=(jax.ShapeDtypeStruct((2 * nblk,),...  3.1 us
  transfers between devices with their start and end apart: 18, of which 7 were waited for; matrix products, arithmetic and copies ran while one was open for 1% of the time, Pallas kernels for 34%

profile of v1, /device:TPU:0, one launch (start us, length us, event | category | flops | bytes accessed | tf_op | source)
XLA Modules:
  0.0 107.8 jit_solution(6955465710959956809)
XLA Ops:
  0.0 3.1 %lead_blocks.1 = (s32[128]{0:T(128)}, bf16[256,2048]{1,0:T(8,128)(2,1)}) custom-call(s32[16]{0:T(128)} %obs_ref.1, bf16[256,8192]{1,0:T(8,128)(2,1)} %ens_ref.3), custom_call_target="tpu_custom_call" | custom-call | tf_op jit(solution)/shard_map/lead_blocks/pallas_call | solution.py:99
  3.1 3.0 %collective-permute-start = (bf16[256,2048]{1,0:T(8,128)(2,1)}, bf16[256,2048]{1,0:T(8,128)(2,1)S(1)}, u32[]{:S(2)}, u32[]{:S(2)}) collective-permute-start(bf16[256,2048]{1,0:T(8,128)(2,1)} %get-tuple-element.61.refs_1_.refs_0_), channel_id=1, source_target_pairs={{0,2},{1,3},{2,0},{3,1},{4,6},{5,7},{6,4},{7,5},{8,10},{9,11},{10,... | collective-permute-start | bytes 3145736 | tf_op jit(solution)/shard_map/ppermute | solution.py:33
  6.2 0.0 copy-start.6
  6.2 0.0 copy-start.7
  6.2 0.0 copy-start.8
  6.2 4.5 %rest_blocks.1 = (bf16[256,3840]{1,0:T(8,128)(2,1)}, bf16[256,2304]{1,0:T(8,128)(2,1)}) custom-call(s32[128]{0:T(128)} %get-tuple-element.57.order_ref, bf16[256,8192]{1,0:T(8,128)(2,1)} %ens_ref.3), custom_call_target="tpu_custom_call" | custom-call | tf_op jit(solution)/shard_map/rest_blocks/pallas_call | solution.py:126
  10.7 0.6 collective-permute-start.6
  11.2 0.1 collective-permute-start.12
  11.4 0.1 broadcast_compare_fusion
  11.4 0.1 select_reduce_fusion
  11.6 0.2 select_reduce_fusion.3
  11.8 0.2 select_reduce_fusion.2
  12.0 18.4 %collective-permute-done.refs_3_.refs_2_ = bf16[256,2048]{1,0:T(8,128)(2,1)S(1)} collective-permute-done((bf16[256,2048]{1,0:T(8,128)(2,1)}, bf16[256,2048]{1,0:T(8,128)(2,1)S(1)}, u32[]{:S(2)}, u32[]{:S(2)}) %collective-permute-start) | collective-permute-done | bytes 1048608 | tf_op jit(solution)/shard_map/ppermute | solution.py:33
  30.3 0.0 collective-permute-done.1.refs_2_.refs_1_
  30.3 0.1 broadcast_in_dim.73
  30.4 0.0 collective-permute-start.2
  30.4 0.5 collective-permute-start.7
  30.9 0.1 pad_add_fusion.refs_0_.index_ref
  31.0 2.9 %collective-permute-done.2.refs_4_.refs_3_ = bf16[256,2048]{1,0:T(8,128)(2,1)} collective-permute-done((bf16[256,2048]{1,0:T(8,128)(2,1)S(1)}, bf16[256,2048]{1,0:T(8,128)(2,1)}, u32[]{:S(2)}, u32[]{:S(2)}) %collective-permute-start.2) | collective-permute-done | bytes 1048608 | tf_op jit(solution)/shard_map/ppermute | solution.py:33
  33.9 4.7 %gram_rows.1 = (bf16[64,1280]{1,0:T(8,128)(2,1)S(1)}, bf16[64,1280]{1,0:T(8,128)(2,1)S(1)}, bf16[64,1152]{1,0:T(8,128)(2,1)S(1)}, bf16[64,1152]{1,0:T(8,128)(2,1)S(1)}) custom-call(s32[2]{0:T(128)S(1)} %pad_add_fusion.refs_0_.index_ref, bf16[256,2048]{1,0:T(8,128)(2,1)S(1)} %copy-done, bf16[256,2048]{1,0:T(8,128)(2,1)S(1)} %collective-permute-done.1.refs_2_.refs_1_, ...), custom_call_target="tpu_custom_call" | custom-call | flops 1024 | bytes 1024 | tf_op jit(solution)/shard_map/gram_rows/pallas_call | solution.py:250
  38.6 2.1 %collective-permute-start.3 = (bf16[64,1280]{1,0:T(8,128)(2,1)S(1)}, bf16[64,1280]{1,0:T(8,128)(2,1)S(1)}, u32[]{:S(2)}, u32[]{:S(2)}) collective-permute-start(bf16[64,1280]{1,0:T(8,128)(2,1)S(1)} %get-tuple-element.73), channel_id=1, source_target_pairs={{0,4},{4,0},{8,12},{12,8},{16,20},{20,16},{24,28},{28,24},{1,5},{5... | collective-permute-start | bytes 491528 | tf_op jit(solution)/shard_map/ppermute | solution.py:33
  40.7 1.8 %sums.3.refs_4_ = f32[1,2048]{1,0:T(1,128)S(1)} custom-call(bf16[256,2048]{1,0:T(8,128)(2,1)S(1)} %copy-done, bf16[256,2048]{1,0:T(8,128)(2,1)S(1)} %collective-permute-done.1.refs_2_.refs_1_, bf16[256,2048]{1,0:T(8,128)(2,1)S(1)} %collective-permute-done.refs_3_.refs_2_, bf16[256,2048]{1,0:T(8,128)(2,1)} %collective-permute-done.2.refs_4_.refs_3_), custom_call_target="tpu_custom_call" | custom-call | flops 1024 | bytes 1024 | tf_op jit(solution)/shard_map/sums/pallas_call | solution.py:503
  42.5 0.0 copy-start.1
  42.6 2.6 %collective-permute-done.3.b_ref = bf16[64,1280]{1,0:T(8,128)(2,1)S(1)} collective-permute-done((bf16[64,1280]{1,0:T(8,128)(2,1)S(1)}, bf16[64,1280]{1,0:T(8,128)(2,1)S(1)}, u32[]{:S(2)}, u32[]{:S(2)}) %collective-permute-start.3) | collective-permute-done | bytes 163872 | tf_op jit(solution)/shard_map/ppermute | solution.py:33
  45.2 1.9 %collective-permute-start.4 = (bf16[64,1280]{1,0:T(8,128)(2,1)S(1)}, bf16[64,1280]{1,0:T(8,128)(2,1)S(1)}, u32[]{:S(2)}, u32[]{:S(2)}) collective-permute-start(bf16[64,1280]{1,0:T(8,128)(2,1)S(1)} %add_slabs.6.a_ref), channel_id=1, source_target_pairs={{0,8},{4,12},{8,0},{12,4},{16,24},{20,28},{24,16},{28,20},{1,9},{5... | collective-permute-start | bytes 491528 | tf_op jit(solution)/shard_map/ppermute | solution.py:33
  47.1 1.5 %collective-permute-start.5 = (bf16[64,1152]{1,0:T(8,128)(2,1)S(1)}, bf16[64,1152]{1,0:T(8,128)(2,1)S(1)}, u32[]{:S(2)}, u32[]{:S(2)}) collective-permute-start(bf16[64,1152]{1,0:T(8,128)(2,1)S(1)} %get-tuple-element.78), channel_id=1, source_target_pairs={{0,4},{4,0},{8,12},{12,8},{16,20},{20,16},{24,28},{28,24},{1,5},{5... | collective-permute-start | bytes 442376 | tf_op jit(solution)/shard_map/ppermute | solution.py:33
  48.6 1.6 %sums.5.refs_4_ = f32[1,2304]{1,0:T(1,128)S(1)} custom-call(bf16[256,2304]{1,0:T(8,128)(2,1)S(1)} %copy-done.2, bf16[256,2304]{1,0:T(8,128)(2,1)} %collective-permute-done.7.refs_1_), custom_call_target="tpu_custom_call" | custom-call | flops 1024 | bytes 1024 | tf_op jit(solution)/shard_map/sums/pallas_call | solution.py:503
  50.2 0.0 collective-permute-done.6.refs_1_
  50.2 2.1 %sums.4.refs_4_ = f32[1,3840]{1,0:T(1,128)S(1)} custom-call(bf16[256,3840]{1,0:T(8,128)(2,1)S(1)} %copy-done.1, bf16[256,3840]{1,0:T(8,128)(2,1)} %collective-permute-done.6.refs_1_), custom_call_target="tpu_custom_call" | custom-call | flops 1024 | bytes 1024 | tf_op jit(solution)/shard_map/sums/pallas_call | solution.py:503
  52.4 0.0 collective-permute-done.4.b_ref
  52.5 2.7 %collective-permute-start.8 = (bf16[64,1280]{1,0:T(8,128)(2,1)S(1)}, bf16[64,1280]{1,0:T(8,128)(2,1)S(1)}, u32[]{:S(2)}, u32[]{:S(2)}) collective-permute-start(bf16[64,1280]{1,0:T(8,128)(2,1)S(1)} %add_slabs.7.a_ref), channel_id=1, source_target_pairs={{0,16},{4,20},{8,24},{12,28},{16,0},{20,4},{24,8},{28,12},{1,17},{... | collective-permute-start | bytes 491528 | tf_op jit(solution)/shard_map/ppermute | solution.py:33
  55.2 0.4 collective-permute-start.9
  55.6 7.2 %collective-permute-done.9.b_ref = bf16[64,1152]{1,0:T(8,128)(2,1)S(1)} collective-permute-done((bf16[64,1152]{1,0:T(8,128)(2,1)S(1)}, bf16[64,1152]{1,0:T(8,128)(2,1)S(1)}, u32[]{:S(2)}, u32[]{:S(2)}) %collective-permute-start.9) | collective-permute-done | bytes 147488 | tf_op jit(solution)/shard_map/ppermute | solution.py:33
  62.9 0.9 collective-permute-start.10
  63.9 7.9 %collective-permute-done.12.refs_2_ = bf16[256,3840]{1,0:T(8,128)(2,1)} collective-permute-done((bf16[256,3840]{1,0:T(8,128)(2,1)}, bf16[256,3840]{1,0:T(8,128)(2,1)}, u32[]{:S(2)}, u32[]{:S(2)}) %collective-permute-start.12) | collective-permute-done | bytes 1966112 | tf_op jit(solution)/shard_map/ppermute | solution.py:33
  71.8 1.8 %collective-permute-start.16 = (bf16[256,2304]{1,0:T(8,128)(2,1)S(1)}, bf16[256,2304]{1,0:T(8,128)(2,1)S(1)}, u32[]{:S(2)}, u32[]{:S(2)}) collective-permute-start(bf16[256,2304]{1,0:T(8,128)(2,1)S(1)} %copy-done.2), channel_id=1, source_target_pairs={{0,2},{1,3},{2,0},{3,1},{4,6},{5,7},{6,4},{7,5},{8,10},{9,11},{10,... | collective-permute-start | bytes 3538952 | tf_op jit(solution)/shard_map/ppermute | solution.py:33
  73.6 1.6 %collective-permute-start.13 = (bf16[64,1152]{1,0:T(8,128)(2,1)S(1)}, bf16[64,1152]{1,0:T(8,128)(2,1)S(1)}, u32[]{:S(2)}, u32[]{:S(2)}) collective-permute-start(bf16[64,1152]{1,0:T(8,128)(2,1)S(1)} %add_slabs.11.two_ref), channel_id=1, source_target_pairs={{0,4},{4,0},{8,12},{12,8},{16,20},{20,16},{24,28},{28,24},{1,5},{5... | collective-permute-start | bytes 442376 | tf_op jit(solution)/shard_map/ppermute | solution.py:33
  75.2 4.4 %collective-permute-done.13.other_two_ref = bf16[64,1152]{1,0:T(8,128)(2,1)S(1)} collective-permute-done((bf16[64,1152]{1,0:T(8,128)(2,1)S(1)}, bf16[64,1152]{1,0:T(8,128)(2,1)S(1)}, u32[]{:S(2)}, u32[]{:S(2)}) %collective-permute-start.13) | collective-permute-done | bytes 147488 | tf_op jit(solution)/shard_map/ppermute | solution.py:33
  79.6 0.6 join_slabs.1.refs_1_
  80.2 0.1 collective-permute-start.14
  80.3 2.1 %collective-permute-done.14.refs_2_ = bf16[256,1280]{1,0:T(8,128)(2,1)S(1)} collective-permute-done((bf16[256,1280]{1,0:T(8,128)(2,1)S(1)}, bf16[256,1280]{1,0:T(8,128)(2,1)S(1)}, u32[]{:S(2)}, u32[]{:S(2)}) %collective-permute-start.14) | collective-permute-done | bytes 655392 | tf_op jit(solution)/shard_map/ppermute | solution.py:33
  82.4 0.0 collective-permute-done.15.refs_3_
  82.4 12.6 %transform_rows.1.t_ref = bf16[256,1024]{1,0:T(8,128)(2,1)S(1)} custom-call(s32[2]{0:T(128)S(1)} %pad_add_fusion.refs_0_.index_ref, bf16[256,1280]{1,0:T(8,128)(2,1)S(1)} %join_slabs.1.refs_1_, bf16[256,1280]{1,0:T(8,128)(2,1)S(1)} %collective-permute-done.14.refs_2_), custom_call_target="tpu_custom_call" | custom-call | flops 1024 | bytes 1024 | tf_op jit(solution)/shard_map/transform_rows/pallas_call | solution.py:475
  95.0 5.5 %update.3.refs_5_ = bf16[256,8192]{1,0:T(8,128)(2,1)} custom-call(s32[128]{0:T(128)S(1)} %copy-done.3, bf16[256,1024]{1,0:T(8,128)(2,1)S(1)} %transform_rows.1.t_ref, f32[1,8192]{1,0:T(1,128)S(1)} %bitcast.12, bf16[256,3840]{1,0:T(8,128)(2,1)S(1)} %copy-done.1, bf16[256,3840]{1,0:T(8,128)(2,1)} %collective-permute-done.6.refs_1_, ...), custom_call_target="tpu_custom_call" | custom-call | flops 1024 | bytes 1024 | tf_op jit(solution)/shard_map/update/pallas_call | solution.py:553
  100.5 0.2 collective-permute-start.17
  100.6 3.3 %update.4.refs_5_ = bf16[256,8192]{1,0:T(8,128)(2,1)} custom-call(s32[128]{0:T(128)S(1)} %copy-done.3, bf16[256,1024]{1,0:T(8,128)(2,1)S(1)} %transform_rows.1.t_ref, f32[1,8192]{1,0:T(1,128)S(1)} %bitcast.13, bf16[256,2048]{1,0:T(8,128)(2,1)S(1)} %copy-done, ...), custom_call_target="tpu_custom_call", output_to_operand_aliasing={{}: (8, {})} | custom-call | flops 1024 | bytes 1024 | tf_op jit(solution)/shard_map/update/pallas_call | solution.py:553
  104.0 0.0 collective-permute-done.17.refs_3_
  104.0 3.6 %update.5 = bf16[256,8192]{1,0:T(8,128)(2,1)} custom-call(s32[128]{0:T(128)S(1)} %copy-done.3, bf16[256,1024]{1,0:T(8,128)(2,1)S(1)} %transform_rows.1.t_ref, f32[1,8192]{1,0:T(1,128)S(1)} %bitcast.14, bf16[256,2304]{1,0:T(8,128)(2,1)S(1)} %copy-done.2, bf16[256,2304]{1,0:T(8,128)(2,1)} %collective-permute-done.7.refs_1_, ...), custom_call_target="tpu_custom_call", output_to_operand_aliasing={{}: (8, {})} | custom-call | flops 1024 | bytes 1024 | tf_op jit(solution)/shard_map/update/pallas_call | solution.py:553
  (32 shorter events, 0.3 us)
Async XLA Ops:
  3.1 27.2 %collective-permute-start = (bf16[256,2048]{1,0:T(8,128)(2,1)}, bf16[256,2048]{1,0:T(8,128)(2,1)S(1)}, u32[]{:S(2)}, u32[]{:S(2)}) collective-permute-start(bf16[256,2048]{1,0:T(8,128)(2,1)} %get-tuple-element.61.refs_1_.refs_0_), channel_id=1, source_target_pairs={{0,2},{1,3},{2,0},{3,1},{4,6},{5,7},{6,4},{7,5},{8,10},{9,11},{10,... | collective-permute-start | bytes 3145736 | tf_op jit(solution)/shard_map/ppermute | solution.py:33
  6.1 24.2 %collective-permute-start.1 = (bf16[256,2048]{1,0:T(8,128)(2,1)}, bf16[256,2048]{1,0:T(8,128)(2,1)S(1)}, u32[]{:S(2)}, u32[]{:S(2)}) collective-permute-start(bf16[256,2048]{1,0:T(8,128)(2,1)} %get-tuple-element.61.refs_1_.refs_0_), channel_id=1, source_target_pairs={{0,1},{1,0},{2,3},{3,2},{4,5},{5,4},{6,7},{7,6},{8,9},{9,8},{10,11... | collective-permute-start | bytes 3145736 | tf_op jit(solution)/shard_map/ppermute | solution.py:33
  6.1 5.2 %copy-start.4 = (f32[2048]{0:T(1024)S(1)}, f32[2048]{0:T(1024)}, u32[]{:S(2)}) copy-start(f32[2048]{0:T(1024)} %param.11) | copy-start | bytes 24580
  6.1 5.2 %copy-start.5 = (f32[2048]{0:T(1024)S(1)}, f32[2048]{0:T(1024)}, u32[]{:S(2)}) copy-start(f32[2048]{0:T(1024)} %param.10) | copy-start | bytes 24580
  6.2 5.2 %copy-start.3 = (s32[128]{0:T(128)S(1)}, s32[128]{0:T(128)}, u32[]{:S(2)}) copy-start(s32[128]{0:T(128)} %get-tuple-element.57.order_ref) | copy-start | bytes 1540
  6.2 5.2 %copy-start.6 = (s32[16]{0:T(128)S(1)}, s32[16]{0:T(128)}, u32[]{:S(2)}) copy-start(s32[16]{0:T(128)} %obs_ref.1) | copy-start | bytes 196
  6.2 5.5 %copy-start.7 = (s32[64]{0:T(128)S(1)}, s32[64]{0:T(128)}, u32[]{:S(2)}) copy-start(s32[64]{0:T(128)} %param.7) | copy-start | bytes 772
  6.2 5.6 %copy-start.8 = (f32[64]{0:T(128)S(1)}, f32[64]{0:T(128)}, u32[]{:S(2)}) copy-start(f32[64]{0:T(128)} %param.8) | copy-start | bytes 772
  6.2 27.7 %copy-start = (bf16[256,2048]{1,0:T(8,128)(2,1)S(1)}, bf16[256,2048]{1,0:T(8,128)(2,1)}, u32[]{:S(2)}) copy-start(bf16[256,2048]{1,0:T(8,128)(2,1)} %get-tuple-element.61.refs_1_.refs_0_) | copy-start | bytes 3145732
  10.7 39.5 %collective-permute-start.6 = (bf16[256,3840]{1,0:T(8,128)(2,1)}, bf16[256,3840]{1,0:T(8,128)(2,1)}, u32[]{:S(2)}, u32[]{:S(2)}) collective-permute-start(bf16[256,3840]{1,0:T(8,128)(2,1)} %get-tuple-element.98.refs_0_), channel_id=1, source_target_pairs={{0,1},{1,0},{2,3},{3,2},{4,5},{5,4},{6,7},{7,6},{8,9},{9,8},{10,11... | collective-permute-start | bytes 5898248 | tf_op jit(solution)/shard_map/ppermute | solution.py:33
  11.2 60.5 %collective-permute-start.12 = (bf16[256,3840]{1,0:T(8,128)(2,1)}, bf16[256,3840]{1,0:T(8,128)(2,1)}, u32[]{:S(2)}, u32[]{:S(2)}) collective-permute-start(bf16[256,3840]{1,0:T(8,128)(2,1)} %get-tuple-element.98.refs_0_), channel_id=1, source_target_pairs={{0,2},{1,3},{2,0},{3,1},{4,6},{5,7},{6,4},{7,5},{8,10},{9,11},{10,... | collective-permute-start | bytes 5898248 | tf_op jit(solution)/shard_map/ppermute | solution.py:33
  30.4 3.5 %collective-permute-start.2 = (bf16[256,2048]{1,0:T(8,128)(2,1)S(1)}, bf16[256,2048]{1,0:T(8,128)(2,1)}, u32[]{:S(2)}, u32[]{:S(2)}) collective-permute-start(bf16[256,2048]{1,0:T(8,128)(2,1)S(1)} %collective-permute-done.refs_3_.refs_2_), channel_id=1, source_target_pairs={{0,1},{1,0},{2,3},{3,2},{4,5},{5,4},{6,7},{7,6},{8,9},{9,8},{10,11... | collective-permute-start | bytes 3145736 | tf_op jit(solution)/shard_map/ppermute | solution.py:33
  30.4 18.2 %collective-permute-start.7 = (bf16[256,2304]{1,0:T(8,128)(2,1)}, bf16[256,2304]{1,0:T(8,128)(2,1)}, u32[]{:S(2)}, u32[]{:S(2)}) collective-permute-start(bf16[256,2304]{1,0:T(8,128)(2,1)} %get-tuple-element.103.refs_0_), channel_id=1, source_target_pairs={{0,1},{1,0},{2,3},{3,2},{4,5},{5,4},{6,7},{7,6},{8,9},{9,8},{10,11... | collective-permute-start | bytes 3538952 | tf_op jit(solution)/shard_map/ppermute | solution.py:33
  38.6 10.0 %copy-start.2 = (bf16[256,2304]{1,0:T(8,128)(2,1)S(1)}, bf16[256,2304]{1,0:T(8,128)(2,1)}, u32[]{:S(2)}) copy-start(bf16[256,2304]{1,0:T(8,128)(2,1)} %get-tuple-element.103.refs_0_) | copy-start | bytes 3538948
  38.6 6.6 %collective-permute-start.3 = (bf16[64,1280]{1,0:T(8,128)(2,1)S(1)}, bf16[64,1280]{1,0:T(8,128)(2,1)S(1)}, u32[]{:S(2)}, u32[]{:S(2)}) collective-permute-start(bf16[64,1280]{1,0:T(8,128)(2,1)S(1)} %get-tuple-element.73), channel_id=1, source_target_pairs={{0,4},{4,0},{8,12},{12,8},{16,20},{20,16},{24,28},{28,24},{1,5},{5... | collective-permute-start | bytes 491528 | tf_op jit(solution)/shard_map/ppermute | solution.py:33
  42.5 7.7 %copy-start.1 = (bf16[256,3840]{1,0:T(8,128)(2,1)S(1)}, bf16[256,3840]{1,0:T(8,128)(2,1)}, u32[]{:S(2)}) copy-start(bf16[256,3840]{1,0:T(8,128)(2,1)} %get-tuple-element.98.refs_0_) | copy-start | bytes 5898244
  45.2 7.2 %collective-permute-start.4 = (bf16[64,1280]{1,0:T(8,128)(2,1)S(1)}, bf16[64,1280]{1,0:T(8,128)(2,1)S(1)}, u32[]{:S(2)}, u32[]{:S(2)}) collective-permute-start(bf16[64,1280]{1,0:T(8,128)(2,1)S(1)} %add_slabs.6.a_ref), channel_id=1, source_target_pairs={{0,8},{4,12},{8,0},{12,4},{16,24},{20,28},{24,16},{28,20},{1,9},{5... | collective-permute-start | bytes 491528 | tf_op jit(solution)/shard_map/ppermute | solution.py:33
  47.1 5.3 %collective-permute-start.5 = (bf16[64,1152]{1,0:T(8,128)(2,1)S(1)}, bf16[64,1152]{1,0:T(8,128)(2,1)S(1)}, u32[]{:S(2)}, u32[]{:S(2)}) collective-permute-start(bf16[64,1152]{1,0:T(8,128)(2,1)S(1)} %get-tuple-element.78), channel_id=1, source_target_pairs={{0,4},{4,0},{8,12},{12,8},{16,20},{20,16},{24,28},{28,24},{1,5},{5... | collective-permute-start | bytes 442376 | tf_op jit(solution)/shard_map/ppermute | solution.py:33
  52.5 10.3 %collective-permute-start.8 = (bf16[64,1280]{1,0:T(8,128)(2,1)S(1)}, bf16[64,1280]{1,0:T(8,128)(2,1)S(1)}, u32[]{:S(2)}, u32[]{:S(2)}) collective-permute-start(bf16[64,1280]{1,0:T(8,128)(2,1)S(1)} %add_slabs.7.a_ref), channel_id=1, source_target_pairs={{0,16},{4,20},{8,24},{12,28},{16,0},{20,4},{24,8},{28,12},{1,17},{... | collective-permute-start | bytes 491528 | tf_op jit(solution)/shard_map/ppermute | solution.py:33
  55.2 7.7 %collective-permute-start.9 = (bf16[64,1152]{1,0:T(8,128)(2,1)S(1)}, bf16[64,1152]{1,0:T(8,128)(2,1)S(1)}, u32[]{:S(2)}, u32[]{:S(2)}) collective-permute-start(bf16[64,1152]{1,0:T(8,128)(2,1)S(1)} %add_slabs.8.a_ref), channel_id=1, source_target_pairs={{0,8},{4,12},{8,0},{12,4},{16,24},{20,28},{24,16},{28,20},{1,9},{5... | collective-permute-start | bytes 442376 | tf_op jit(solution)/shard_map/ppermute | solution.py:33
  62.9 8.8 %collective-permute-start.10 = (bf16[64,1280]{1,0:T(8,128)(2,1)S(1)}, bf16[64,1280]{1,0:T(8,128)(2,1)S(1)}, u32[]{:S(2)}, u32[]{:S(2)}) collective-permute-start(bf16[64,1280]{1,0:T(8,128)(2,1)S(1)} %add_slabs.9.one_ref), channel_id=1, source_target_pairs={{0,4},{4,0},{8,12},{12,8},{16,20},{20,16},{24,28},{28,24},{1,5},{5... | collective-permute-start | bytes 491528 | tf_op jit(solution)/shard_map/ppermute | solution.py:33
  63.9 7.9 %collective-permute-start.11 = (bf16[64,1152]{1,0:T(8,128)(2,1)S(1)}, bf16[64,1152]{1,0:T(8,128)(2,1)S(1)}, u32[]{:S(2)}, u32[]{:S(2)}) collective-permute-start(bf16[64,1152]{1,0:T(8,128)(2,1)S(1)} %add_slabs.10.a_ref), channel_id=1, source_target_pairs={{0,16},{4,20},{8,24},{12,28},{16,0},{20,4},{24,8},{28,12},{1,17},{... | collective-permute-start | bytes 442376 | tf_op jit(solution)/shard_map/ppermute | solution.py:33
  71.8 10.6 %collective-permute-start.15 = (bf16[256,3840]{1,0:T(8,128)(2,1)}, bf16[256,3840]{1,0:T(8,128)(2,1)S(1)}, u32[]{:S(2)}, u32[]{:S(2)}) collective-permute-start(bf16[256,3840]{1,0:T(8,128)(2,1)} %collective-permute-done.12.refs_2_), channel_id=1, source_target_pairs={{0,1},{1,0},{2,3},{3,2},{4,5},{5,4},{6,7},{7,6},{8,9},{9,8},{10,11... | collective-permute-start | bytes 5898248 | tf_op jit(solution)/shard_map/ppermute | solution.py:33
  71.8 28.7 %collective-permute-start.16 = (bf16[256,2304]{1,0:T(8,128)(2,1)S(1)}, bf16[256,2304]{1,0:T(8,128)(2,1)S(1)}, u32[]{:S(2)}, u32[]{:S(2)}) collective-permute-start(bf16[256,2304]{1,0:T(8,128)(2,1)S(1)} %copy-done.2), channel_id=1, source_target_pairs={{0,2},{1,3},{2,0},{3,1},{4,6},{5,7},{6,4},{7,5},{8,10},{9,11},{10,... | collective-permute-start | bytes 3538952 | tf_op jit(solution)/shard_map/ppermute | solution.py:33
  73.6 6.0 %collective-permute-start.13 = (bf16[64,1152]{1,0:T(8,128)(2,1)S(1)}, bf16[64,1152]{1,0:T(8,128)(2,1)S(1)}, u32[]{:S(2)}, u32[]{:S(2)}) collective-permute-start(bf16[64,1152]{1,0:T(8,128)(2,1)S(1)} %add_slabs.11.two_ref), channel_id=1, source_target_pairs={{0,4},{4,0},{8,12},{12,8},{16,20},{20,16},{24,28},{28,24},{1,5},{5... | collective-permute-start | bytes 442376 | tf_op jit(solution)/shard_map/ppermute | solution.py:33
  80.2 2.2 %collective-permute-start.14 = (bf16[256,1280]{1,0:T(8,128)(2,1)S(1)}, bf16[256,1280]{1,0:T(8,128)(2,1)S(1)}, u32[]{:S(2)}, u32[]{:S(2)}) collective-permute-start(bf16[256,1280]{1,0:T(8,128)(2,1)S(1)} %join_slabs.1.refs_1_), channel_id=1, source_target_pairs={{0,1},{1,0},{2,3},{3,2},{4,5},{5,4},{6,7},{7,6},{8,9},{9,8},{10,11... | collective-permute-start | bytes 1966088 | tf_op jit(solution)/shard_map/ppermute | solution.py:33
  100.5 3.5 %collective-permute-start.17 = (bf16[256,2304]{1,0:T(8,128)(2,1)S(1)}, bf16[256,2304]{1,0:T(8,128)(2,1)S(1)}, u32[]{:S(2)}, u32[]{:S(2)}) collective-permute-start(bf16[256,2304]{1,0:T(8,128)(2,1)S(1)} %collective-permute-done.16.refs_2_), channel_id=1, source_target_pairs={{0,1},{1,0},{2,3},{3,2},{4,5},{5,4},{6,7},{7,6},{8,9},{9,8},{10,11... | collective-permute-start | bytes 3538952 | tf_op jit(solution)/shard_map/ppermute | solution.py:33

commit v2 on v1

--- a/solution.py
+++ b/solution.py
@@ -176,14 +176,10 @@
     for first in range(0, cols, width):
         part = slice(first, first + width)
         factor = factor_ref[:, part]
-        values = [r[:, part].astype(F32) for r in raws]
-        total = jnp.sum(values[0], axis=0, keepdims=True)
-        for v in values[1:]:
-            total = total + jnp.sum(v, axis=0, keepdims=True)
-        mean = total / (local * parts)
+        mean = column_sums([r[:, part] for r in raws]) / (local * parts)
         both = factor * root_ref[:, part]
-        for m, v in enumerate(values):
-            v = v - mean
+        for m, r in enumerate(raws):
+            v = r[:, part].astype(F32) - mean
             place = (m % 2 * count + m // 2) * local
             scaled[place : place + local, part] = (both * v).astype(BF16)
             if m % 2 == 0:
@@ -313,8 +309,8 @@
 
 
 def root_kernel(parts, scale_root, tile, *refs):
-    index_ref, mine_ref, sibling_ref, out_ref = refs[:4]
-    u, ub, rest, rb, work, wb, wb2, tail = refs[4:]
+    index_ref, mine_ref, sibling_ref, out_ref, sums_ref = refs[:5]
+    u, ub, rest, rb, wb, wb2, tail = refs[5:]
     members = u.shape[0]
     local = members // parts
     half = local // 2
@@ -382,13 +378,11 @@
             ref[col, first : first + tile] = block.T
 
     inverse = 1.0 / frob
-    unit = u[...] * inverse
-    u[...] = unit
-    ub[:members, :] = unit.astype(BF16)
+    ub[:members, :] = (u[...] * inverse).astype(BF16)
 
     def square_columns(below, col):
         v = dot(ub[below, :], ub[:members, col])
-        unit = u[below, col]
+        unit = u[below, col] * inverse
         mirror(wb, below, col, v)
         mirror(wb2, below, col, 0.0625 * v - 0.5625 * unit)
         rest[below, col] = 1.6875 * v - 2.4375 * unit
@@ -413,13 +407,12 @@
 
     def z_columns(below, col):
         y = dot(ub[below.start :, :], rb[:members, col])
-        z = 2.25 * u[below, col] + y[:-PAD]
+        z = (2.25 * inverse) * u[below, col] + y[:-PAD]
         tail[:, col] = y[-PAD:]
-        work[below, col] = z
         mirror(wb, below, col, z)
 
     def a_columns(below, col):
-        a = 2.25 * work[below, col] + dot(wb[below, :], rb[:members, col])
+        a = 2.25 * wb[below, col].astype(F32) + dot(wb[below, :], rb[:members, col])
         mirror(wb2, below, col, a)
         rest[below, col] = 1.5 * rest[below, col] - 1.125 * a
 
@@ -448,7 +441,7 @@
     unit_cols = ub[:members, :]
     rest_cols = wb[...]
     y, z_row = times(rest_rows, third_row, unit_cols)
-    z = 3.375 * u[:local, :] + y
+    z = (3.375 * inverse) * u[:local, :] + y
     y, a_row = times(z, z_row, rest_cols)
     a, a_row = 3.375 * z + y, 3.375 * z_row + a_row
     y, b_row = times(a, a_row, rest_cols)
@@ -463,7 +456,10 @@
     a_row = 3.375 * z_row + row_times(z_row, rest_cols)
     b_row = 3.375 * a_row + row_times(a_row, rest_cols)
     shift = (1.5 * y_row - 0.5 * b_row) * (inverse / scale_root)
-    out_ref[...] = (fourth * jnp.sqrt(inverse) + shift).astype(BF16)
+    transform = (fourth * jnp.sqrt(inverse) + shift).astype(BF16)
+    out_ref[...] = transform
+    row_sums = jnp.sum(transform.astype(F32), axis=1, keepdims=True)
+    sums_ref[...] = jnp.broadcast_to(row_sums, sums_ref.shape)
 
 
 def transform_rows(index, mine, sibling, parts, scale_root, tile=256):
@@ -474,10 +470,13 @@
     longer = pltpu.VMEM((members + PAD, members), BF16)
     return pl.pallas_call(
         functools.partial(root_kernel, parts, scale_root, tile),
-        out_shape=jax.ShapeDtypeStruct((local, members), BF16),
+        out_shape=(
+            jax.ShapeDtypeStruct((local, members), BF16),
+            jax.ShapeDtypeStruct((local, LANES), F32),
+        ),
         in_specs=[SMEM] + [VMEM] * 2,
-        out_specs=VMEM,
-        scratch_shapes=[wide, longer, wide, longer, wide, narrow, narrow]
+        out_specs=(VMEM, VMEM),
+        scratch_shapes=[wide, longer, wide, longer, narrow, narrow]
         + [pltpu.VMEM((PAD, members), F32)],
         compiler_params=pltpu.CompilerParams(vmem_limit_bytes=36 * MIB),
         cost_estimate=pl.CostEstimate(flops=1024, bytes_accessed=1024, transcendentals=0),
@@ -511,11 +510,11 @@
     )(*pieces)
 
 
-def update_kernel(width, parts, start, summed, order_ref, t_ref, factor_ref, *refs):
+def update_kernel(width, parts, start, summed, order_ref, t_ref, rows_ref, factor_ref, *refs):
     raws, totals = refs[: parts * len(summed)], refs[parts * len(summed) : (parts + 1) * len(summed)]
     out_ref, buf, sem = refs[-3:]
     local, members = t_ref.shape
-    rows = jnp.sum(t_ref[...].astype(F32), axis=1, keepdims=True)
+    rows = rows_ref[:, :1]
     col = 0
     for chunk, (done, total_ref) in enumerate(zip(summed, totals)):
         held = raws[chunk * parts : (chunk + 1) * parts]
@@ -528,7 +527,9 @@
                 total = total + column_sums(pieces[done:])
             mean = total / members
             factor = factor_ref[:, start + col : start + col + count]
-            product = dot(t_ref[...], jnp.concatenate(pieces, axis=0))
+            product = dot(t_ref[:, :local], held[0][:, part])
+            for m in range(1, parts):
+                product += dot(t_ref[:, m * local : (m + 1) * local], held[m][:, part])
             buf[:, col : col + count] = (
                 factor * product + (mean - (mean * factor) * rows)
             ).astype(BF16)
@@ -542,8 +543,8 @@
     pltpu.make_async_copy(buf, out_ref.at[:, pl.ds(0, col)], sem).wait()
 
 
-def update(order, transform, factor, chunks, totals, summed, start, result=None, width=512):
-    local, members = transform.shape
+def update(order, transform, factor, chunks, totals, summed, start, result=None, width=1024):
+    local = transform[0].shape[0]
     parts = len(chunks[0])
     states = factor.shape[1]
     cols = sum(raws[0].shape[1] for raws in chunks)
@@ -553,14 +554,14 @@
     return pl.pallas_call(
         functools.partial(update_kernel, width, parts, start, summed),
         out_shape=jax.ShapeDtypeStruct((local, states), BF16),
-        in_specs=[SMEM, VMEM, VMEM] + [VMEM] * len(inputs) + [ANY] * len(extra),
+        in_specs=[SMEM, VMEM, VMEM, VMEM] + [VMEM] * len(inputs) + [ANY] * len(extra),
         out_specs=ANY,
         scratch_shapes=[pltpu.VMEM((local, cols), BF16), pltpu.SemaphoreType.DMA],
-        input_output_aliases={3 + len(inputs): 0} if extra else {},
+        input_output_aliases={4 + len(inputs): 0} if extra else {},
         compiler_params=pltpu.CompilerParams(vmem_limit_bytes=24 * MIB),
         cost_estimate=pl.CostEstimate(flops=1024, bytes_accessed=1024, transcendentals=0),
         name="update",
-    )(order, transform, factor, *inputs, *extra)
+    )(order, *transform, factor, *inputs, *extra)
 
 
 def on_device(ensemble, owner, inflation, obs_block, obs_value, obs_std):
@@ -574,7 +575,7 @@
     order, lead = lead_blocks(obs_block, ensemble, nob)
     lead_far = far(lead)
     left = nblk - nob
-    sizes = [left * 30 // 48]
+    sizes = [left * 33 // 48]
     sizes.append(left - sum(sizes))
     starts = [nob * CLASSES]
     for n in sizes[:-1]:
@@ -623,7 +624,7 @@
         elif slot == 1:
             early = [sums([chunk, own]) for chunk, own in zip(rest, owns)]
             got, early, owns = tie(got, early, owns)
-        elif slot == len(steps) - 1:
+        elif slot == len(steps):
             got, fars[0] = tie(got, fars[0])
         else:
             (got,) = tie(got)

time: 108 us -> 108 us (level)
  transfers between devices with their start and end apart: 18 -> 18, of which waited for: 7 -> 9; matrix products, arithmetic and copies ran while one was open for 1% -> 1% of each run, Pallas kernels for 34% -> 34%
where the time goes in v2:
time: 108 us
  waiting for transfers between devices  46.2 us (43%)
  Pallas kernels  43.4 us (40%)
  starting transfers between devices  16.7 us (15%)
    ppermute x18, waiting for transfers between devices, swap(): return lax.ppermute(x, axis, [(i, i ^ mask) for i in range(size)])  46.2 us
    ppermute x18, starting transfers between devices, swap(): return lax.ppermute(x, axis, [(i, i ^ mask) for i in range(size)])  16.7 us
    pallas_call x3, Pallas kernels, update(): pl.pallas_call(functools.partial(update_kernel, width, parts, start, summ...  12.5 us
    pallas_call x1, Pallas kernels, transform_rows(): pl.pallas_call(functools.partial(root_kernel, parts, scale_root, tile), o...  12.4 us
    pallas_call x3, Pallas kernels, sums(): pl.pallas_call(functools.partial(sums_kernel, width), out_shape=jax.Shape...  5.62 us
    pallas_call x1, Pallas kernels, gram_rows(): pl.pallas_call(functools.partial(gram_kernel, parts, scale_root, width),...  4.34 us
    pallas_call x1, Pallas kernels, rest_blocks(): pl.pallas_call(functools.partial(rest_kernel, lead), out_shape=[jax.Shape...  4.34 us
    pallas_call x1, Pallas kernels, lead_blocks(): pl.pallas_call(lead_kernel, out_shape=(jax.ShapeDtypeStruct((2 * nblk,),...  3.26 us
  transfers between devices with their start and end apart: 18, of which 9 were waited for; matrix products, arithmetic and copies ran while one was open for 1% of the time, Pallas kernels for 34%

profile of v2, /device:TPU:0, one launch (start us, length us, event | category | flops | bytes accessed | tf_op | source)
XLA Modules:
  0.0 107.5 jit_solution(8763080290830998022)
XLA Ops:
  0.0 3.3 %lead_blocks.1 = (s32[128]{0:T(128)}, bf16[256,2048]{1,0:T(8,128)(2,1)}) custom-call(s32[16]{0:T(128)} %obs_ref.1, bf16[256,8192]{1,0:T(8,128)(2,1)} %ens_ref.3), custom_call_target="tpu_custom_call" | custom-call | tf_op jit(solution)/shard_map/lead_blocks/pallas_call | solution.py:99
  3.3 3.0 %collective-permute-start = (bf16[256,2048]{1,0:T(8,128)(2,1)}, bf16[256,2048]{1,0:T(8,128)(2,1)S(1)}, u32[]{:S(2)}, u32[]{:S(2)}) collective-permute-start(bf16[256,2048]{1,0:T(8,128)(2,1)} %get-tuple-element.64.refs_1_.refs_0_), channel_id=1, source_target_pairs={{0,2},{1,3},{2,0},{3,1},{4,6},{5,7},{6,4},{7,5},{8,10},{9,11},{10,... | collective-permute-start | bytes 3145736 | tf_op jit(solution)/shard_map/ppermute | solution.py:33
  6.4 4.3 %rest_blocks.1 = (bf16[256,4224]{1,0:T(8,128)(2,1)}, bf16[256,1920]{1,0:T(8,128)(2,1)}) custom-call(s32[128]{0:T(128)} %get-tuple-element.60.order_ref, bf16[256,8192]{1,0:T(8,128)(2,1)} %ens_ref.3), custom_call_target="tpu_custom_call" | custom-call | tf_op jit(solution)/shard_map/rest_blocks/pallas_call | solution.py:126
  10.7 0.6 collective-permute-start.6
  11.3 0.1 collective-permute-start.13
  11.4 0.1 broadcast_compare_fusion
  11.5 0.1 select_reduce_fusion
  11.7 0.2 select_reduce_fusion.3
  11.8 0.2 select_reduce_fusion.2
  12.0 18.5 %collective-permute-done.refs_3_.refs_2_ = bf16[256,2048]{1,0:T(8,128)(2,1)S(1)} collective-permute-done((bf16[256,2048]{1,0:T(8,128)(2,1)}, bf16[256,2048]{1,0:T(8,128)(2,1)S(1)}, u32[]{:S(2)}, u32[]{:S(2)}) %collective-permute-start) | collective-permute-done | bytes 1048608 | tf_op jit(solution)/shard_map/ppermute | solution.py:33
  30.6 0.0 collective-permute-done.1.refs_2_.refs_1_
  30.6 0.1 broadcast_in_dim.73
  30.6 0.0 collective-permute-start.2
  30.6 0.5 collective-permute-start.7
  31.1 0.1 pad_add_fusion.refs_0_.index_ref
  31.2 2.9 %collective-permute-done.2.refs_4_.refs_3_ = bf16[256,2048]{1,0:T(8,128)(2,1)} collective-permute-done((bf16[256,2048]{1,0:T(8,128)(2,1)S(1)}, bf16[256,2048]{1,0:T(8,128)(2,1)}, u32[]{:S(2)}, u32[]{:S(2)}) %collective-permute-start.2) | collective-permute-done | bytes 1048608 | tf_op jit(solution)/shard_map/ppermute | solution.py:33
  34.1 4.3 %gram_rows.1 = (bf16[64,1280]{1,0:T(8,128)(2,1)S(1)}, bf16[64,1280]{1,0:T(8,128)(2,1)S(1)}, bf16[64,1152]{1,0:T(8,128)(2,1)S(1)}, bf16[64,1152]{1,0:T(8,128)(2,1)S(1)}) custom-call(s32[2]{0:T(128)S(1)} %pad_add_fusion.refs_0_.index_ref, bf16[256,2048]{1,0:T(8,128)(2,1)S(1)} %copy-done, bf16[256,2048]{1,0:T(8,128)(2,1)S(1)} %collective-permute-done.1.refs_2_.refs_1_, ...), custom_call_target="tpu_custom_call" | custom-call | flops 1024 | bytes 1024 | tf_op jit(solution)/shard_map/gram_rows/pallas_call | solution.py:246
  38.5 0.0 copy-start.1
  38.5 2.1 %collective-permute-start.3 = (bf16[64,1280]{1,0:T(8,128)(2,1)S(1)}, bf16[64,1280]{1,0:T(8,128)(2,1)S(1)}, u32[]{:S(2)}, u32[]{:S(2)}) collective-permute-start(bf16[64,1280]{1,0:T(8,128)(2,1)S(1)} %get-tuple-element.76), channel_id=1, source_target_pairs={{0,4},{4,0},{8,12},{12,8},{16,20},{20,16},{24,28},{28,24},{1,5},{5... | collective-permute-start | bytes 491528 | tf_op jit(solution)/shard_map/ppermute | solution.py:33
  40.6 1.8 %sums.3.refs_4_ = f32[1,2048]{1,0:T(1,128)S(1)} custom-call(bf16[256,2048]{1,0:T(8,128)(2,1)S(1)} %copy-done, bf16[256,2048]{1,0:T(8,128)(2,1)S(1)} %collective-permute-done.1.refs_2_.refs_1_, bf16[256,2048]{1,0:T(8,128)(2,1)S(1)} %collective-permute-done.refs_3_.refs_2_, bf16[256,2048]{1,0:T(8,128)(2,1)} %collective-permute-done.2.refs_4_.refs_3_), custom_call_target="tpu_custom_call" | custom-call | flops 1024 | bytes 1024 | tf_op jit(solution)/shard_map/sums/pallas_call | solution.py:502
  42.4 2.6 %collective-permute-done.3.b_ref = bf16[64,1280]{1,0:T(8,128)(2,1)S(1)} collective-permute-done((bf16[64,1280]{1,0:T(8,128)(2,1)S(1)}, bf16[64,1280]{1,0:T(8,128)(2,1)S(1)}, u32[]{:S(2)}, u32[]{:S(2)}) %collective-permute-start.3) | collective-permute-done | bytes 163872 | tf_op jit(solution)/shard_map/ppermute | solution.py:33
  45.1 1.9 %collective-permute-start.4 = (bf16[64,1280]{1,0:T(8,128)(2,1)S(1)}, bf16[64,1280]{1,0:T(8,128)(2,1)S(1)}, u32[]{:S(2)}, u32[]{:S(2)}) collective-permute-start(bf16[64,1280]{1,0:T(8,128)(2,1)S(1)} %add_slabs.6.a_ref), channel_id=1, source_target_pairs={{0,8},{4,12},{8,0},{12,4},{16,24},{20,28},{24,16},{28,20},{1,9},{5... | collective-permute-start | bytes 491528 | tf_op jit(solution)/shard_map/ppermute | solution.py:33
  47.0 1.5 %collective-permute-start.5 = (bf16[64,1152]{1,0:T(8,128)(2,1)S(1)}, bf16[64,1152]{1,0:T(8,128)(2,1)S(1)}, u32[]{:S(2)}, u32[]{:S(2)}) collective-permute-start(bf16[64,1152]{1,0:T(8,128)(2,1)S(1)} %get-tuple-element.81), channel_id=1, source_target_pairs={{0,4},{4,0},{8,12},{12,8},{16,20},{20,16},{24,28},{28,24},{1,5},{5... | collective-permute-start | bytes 442376 | tf_op jit(solution)/shard_map/ppermute | solution.py:33
  48.4 0.0 collective-permute-done.7.refs_1_
  48.5 1.5 %sums.5.refs_4_ = f32[1,1920]{1,0:T(1,128)S(1)} custom-call(bf16[256,1920]{1,0:T(8,128)(2,1)S(1)} %copy-done.2, bf16[256,1920]{1,0:T(8,128)(2,1)} %collective-permute-done.7.refs_1_), custom_call_target="tpu_custom_call" | custom-call | flops 1024 | bytes 1024 | tf_op jit(solution)/shard_map/sums/pallas_call | solution.py:502
  50.0 0.0 collective-permute-done.6.refs_1_
  50.0 2.3 %sums.4.refs_4_ = f32[1,4224]{1,0:T(1,128)S(1)} custom-call(bf16[256,4224]{1,0:T(8,128)(2,1)S(1)} %copy-done.1, bf16[256,4224]{1,0:T(8,128)(2,1)} %collective-permute-done.6.refs_1_), custom_call_target="tpu_custom_call" | custom-call | flops 1024 | bytes 1024 | tf_op jit(solution)/shard_map/sums/pallas_call | solution.py:502
  52.2 0.0 collective-permute-done.5.b_ref
  52.3 0.0 collective-permute-done.4.b_ref
  52.4 2.6 %collective-permute-start.8 = (bf16[64,1280]{1,0:T(8,128)(2,1)S(1)}, bf16[64,1280]{1,0:T(8,128)(2,1)S(1)}, u32[]{:S(2)}, u32[]{:S(2)}) collective-permute-start(bf16[64,1280]{1,0:T(8,128)(2,1)S(1)} %add_slabs.7.a_ref), channel_id=1, source_target_pairs={{0,16},{4,20},{8,24},{12,28},{16,0},{20,4},{24,8},{28,12},{1,17},{... | collective-permute-start | bytes 491528 | tf_op jit(solution)/shard_map/ppermute | solution.py:33
  55.0 0.5 collective-permute-start.9
  55.5 7.2 %collective-permute-done.9.b_ref = bf16[64,1152]{1,0:T(8,128)(2,1)S(1)} collective-permute-done((bf16[64,1152]{1,0:T(8,128)(2,1)S(1)}, bf16[64,1152]{1,0:T(8,128)(2,1)S(1)}, u32[]{:S(2)}, u32[]{:S(2)}) %collective-permute-start.9) | collective-permute-done | bytes 147488 | tf_op jit(solution)/shard_map/ppermute | solution.py:33
  62.8 0.9 collective-permute-start.10
  63.7 7.5 %collective-permute-done.11.b_ref = bf16[64,1152]{1,0:T(8,128)(2,1)S(1)} collective-permute-done((bf16[64,1152]{1,0:T(8,128)(2,1)S(1)}, bf16[64,1152]{1,0:T(8,128)(2,1)S(1)}, u32[]{:S(2)}, u32[]{:S(2)}) %collective-permute-start.11) | collective-permute-done | bytes 147488 | tf_op jit(solution)/shard_map/ppermute | solution.py:33
  71.2 0.0 collective-permute-done.10.other_one_ref
  71.3 1.2 %collective-permute-start.12 = (bf16[64,1152]{1,0:T(8,128)(2,1)S(1)}, bf16[64,1152]{1,0:T(8,128)(2,1)S(1)}, u32[]{:S(2)}, u32[]{:S(2)}) collective-permute-start(bf16[64,1152]{1,0:T(8,128)(2,1)S(1)} %add_slabs.11.two_ref), channel_id=1, source_target_pairs={{0,4},{4,0},{8,12},{12,8},{16,20},{20,16},{24,28},{28,24},{1,5},{5... | collective-permute-start | bytes 442376 | tf_op jit(solution)/shard_map/ppermute | solution.py:33
  72.4 3.7 %collective-permute-done.13.refs_2_ = bf16[256,4224]{1,0:T(8,128)(2,1)} collective-permute-done((bf16[256,4224]{1,0:T(8,128)(2,1)}, bf16[256,4224]{1,0:T(8,128)(2,1)}, u32[]{:S(2)}, u32[]{:S(2)}) %collective-permute-start.13) | collective-permute-done | bytes 2162720 | tf_op jit(solution)/shard_map/ppermute | solution.py:33
  76.2 0.3 collective-permute-done.12.other_two_ref
  76.5 1.5 %collective-permute-start.16 = (bf16[256,1920]{1,0:T(8,128)(2,1)S(1)}, bf16[256,1920]{1,0:T(8,128)(2,1)S(1)}, u32[]{:S(2)}, u32[]{:S(2)}) collective-permute-start(bf16[256,1920]{1,0:T(8,128)(2,1)S(1)} %copy-done.2), channel_id=1, source_target_pairs={{0,2},{1,3},{2,0},{3,1},{4,6},{5,7},{6,4},{7,5},{8,10},{9,11},{10,... | collective-permute-start | bytes 2949128 | tf_op jit(solution)/shard_map/ppermute | solution.py:33
  78.0 0.6 join_slabs.1.refs_1_
  78.6 0.3 collective-permute-start.14
  78.9 2.8 %collective-permute-done.14.refs_2_ = bf16[256,1280]{1,0:T(8,128)(2,1)S(1)} collective-permute-done((bf16[256,1280]{1,0:T(8,128)(2,1)S(1)}, bf16[256,1280]{1,0:T(8,128)(2,1)S(1)}, u32[]{:S(2)}, u32[]{:S(2)}) %collective-permute-start.14) | collective-permute-done | bytes 655392 | tf_op jit(solution)/shard_map/ppermute | solution.py:33
  81.7 12.4 %transform_rows.1 = (bf16[256,1024]{1,0:T(8,128)(2,1)S(1)}, f32[256,128]{1,0:T(8,128)S(1)}) custom-call(s32[2]{0:T(128)S(1)} %pad_add_fusion.refs_0_.index_ref, bf16[256,1280]{1,0:T(8,128)(2,1)S(1)} %join_slabs.1.refs_1_, bf16[256,1280]{1,0:T(8,128)(2,1)S(1)} %collective-permute-done.14.refs_2_), custom_call_target="tpu_custom_call" | custom-call | flops 1024 | bytes 1024 | tf_op jit(solution)/shard_map/transform_rows/pallas_call | solution.py:471
  94.1 5.8 %update.3.refs_5_ = bf16[256,8192]{1,0:T(8,128)(2,1)} custom-call(s32[128]{0:T(128)S(1)} %copy-done.3, bf16[256,1024]{1,0:T(8,128)(2,1)S(1)} %get-tuple-element.102.t_ref, f32[256,128]{1,0:T(8,128)S(1)} %get-tuple-element.103.rows_ref, f32[1,8192]{1,0:T(1,128)S(1)} %bitcast.12, bf16[256,4224]{1,0:T(8,128)(2,1)S(1)} %copy-done.1, ...), custom_call_target="tpu_custom_call" | custom-call | flops 1024 | bytes 1024 | tf_op jit(solution)/shard_map/update/pallas_call | solution.py:554
  99.9 0.7 collective-permute-done.16.refs_2_
  100.6 0.0 collective-permute-start.17
  100.6 3.4 %update.4.refs_5_ = bf16[256,8192]{1,0:T(8,128)(2,1)} custom-call(s32[128]{0:T(128)S(1)} %copy-done.3, bf16[256,1024]{1,0:T(8,128)(2,1)S(1)} %get-tuple-element.102.t_ref, f32[256,128]{1,0:T(8,128)S(1)} %get-tuple-element.103.rows_ref, f32[1,8192]{1,0:T(1,128)S(1)} %bitcast.13, bf16[256,2048]{1,0:T(8,128)(2,1)S(1)} %copy-done, ...), custom_call_target="tpu_custom_call", output_to_operand_aliasing={{}: (9, {})} | custom-call | flops 1024 | bytes 1024 | tf_op jit(solution)/shard_map/update/pallas_call | solution.py:554
  104.0 3.3 %update.5 = bf16[256,8192]{1,0:T(8,128)(2,1)} custom-call(s32[128]{0:T(128)S(1)} %copy-done.3, bf16[256,1024]{1,0:T(8,128)(2,1)S(1)} %get-tuple-element.102.t_ref, f32[256,128]{1,0:T(8,128)S(1)} %get-tuple-element.103.rows_ref, f32[1,8192]{1,0:T(1,128)S(1)} %bitcast.14, bf16[256,1920]{1,0:T(8,128)(2,1)S(1)} %copy-done.2, ...), custom_call_target="tpu_custom_call", output_to_operand_aliasing={{}: (9, {})} | custom-call | flops 1024 | bytes 1024 | tf_op jit(solution)/shard_map/update/pallas_call | solution.py:554
  (32 shorter events, 0.3 us)
Async XLA Ops:
  0.0 11.4 %copy-start.6 = (s32[16]{0:T(128)S(1)}, s32[16]{0:T(128)}, u32[]{:S(2)}) copy-start(s32[16]{0:T(128)} %obs_ref.1) | copy-start | bytes 196
  0.0 11.4 %copy-start.5 = (f32[2048]{0:T(1024)S(1)}, f32[2048]{0:T(1024)}, u32[]{:S(2)}) copy-start(f32[2048]{0:T(1024)} %param.10) | copy-start | bytes 24580
  0.0 11.4 %copy-start.4 = (f32[2048]{0:T(1024)S(1)}, f32[2048]{0:T(1024)}, u32[]{:S(2)}) copy-start(f32[2048]{0:T(1024)} %param.11) | copy-start | bytes 24580
  0.0 11.6 %copy-start.7 = (s32[64]{0:T(128)S(1)}, s32[64]{0:T(128)}, u32[]{:S(2)}) copy-start(s32[64]{0:T(128)} %param.7) | copy-start | bytes 772
  0.0 11.8 %copy-start.8 = (f32[64]{0:T(128)S(1)}, f32[64]{0:T(128)}, u32[]{:S(2)}) copy-start(f32[64]{0:T(128)} %param.8) | copy-start | bytes 772
  3.3 8.1 %copy-start.3 = (s32[128]{0:T(128)S(1)}, s32[128]{0:T(128)}, u32[]{:S(2)}) copy-start(s32[128]{0:T(128)} %get-tuple-element.60.order_ref) | copy-start | bytes 1540
  3.3 30.8 %copy-start = (bf16[256,2048]{1,0:T(8,128)(2,1)S(1)}, bf16[256,2048]{1,0:T(8,128)(2,1)}, u32[]{:S(2)}) copy-start(bf16[256,2048]{1,0:T(8,128)(2,1)} %get-tuple-element.64.refs_1_.refs_0_) | copy-start | bytes 3145732
  3.3 27.2 %collective-permute-start = (bf16[256,2048]{1,0:T(8,128)(2,1)}, bf16[256,2048]{1,0:T(8,128)(2,1)S(1)}, u32[]{:S(2)}, u32[]{:S(2)}) collective-permute-start(bf16[256,2048]{1,0:T(8,128)(2,1)} %get-tuple-element.64.refs_1_.refs_0_), channel_id=1, source_target_pairs={{0,2},{1,3},{2,0},{3,1},{4,6},{5,7},{6,4},{7,5},{8,10},{9,11},{10,... | collective-permute-start | bytes 3145736 | tf_op jit(solution)/shard_map/ppermute | solution.py:33
  6.4 24.2 %collective-permute-start.1 = (bf16[256,2048]{1,0:T(8,128)(2,1)}, bf16[256,2048]{1,0:T(8,128)(2,1)S(1)}, u32[]{:S(2)}, u32[]{:S(2)}) collective-permute-start(bf16[256,2048]{1,0:T(8,128)(2,1)} %get-tuple-element.64.refs_1_.refs_0_), channel_id=1, source_target_pairs={{0,1},{1,0},{2,3},{3,2},{4,5},{5,4},{6,7},{7,6},{8,9},{9,8},{10,11... | collective-permute-start | bytes 3145736 | tf_op jit(solution)/shard_map/ppermute | solution.py:33
  10.7 39.3 %collective-permute-start.6 = (bf16[256,4224]{1,0:T(8,128)(2,1)}, bf16[256,4224]{1,0:T(8,128)(2,1)}, u32[]{:S(2)}, u32[]{:S(2)}) collective-permute-start(bf16[256,4224]{1,0:T(8,128)(2,1)} %get-tuple-element.104.refs_0_), channel_id=1, source_target_pairs={{0,1},{1,0},{2,3},{3,2},{4,5},{5,4},{6,7},{7,6},{8,9},{9,8},{10,11... | collective-permute-start | bytes 6488072 | tf_op jit(solution)/shard_map/ppermute | solution.py:33
  11.3 64.9 %collective-permute-start.13 = (bf16[256,4224]{1,0:T(8,128)(2,1)}, bf16[256,4224]{1,0:T(8,128)(2,1)}, u32[]{:S(2)}, u32[]{:S(2)}) collective-permute-start(bf16[256,4224]{1,0:T(8,128)(2,1)} %get-tuple-element.104.refs_0_), channel_id=1, source_target_pairs={{0,2},{1,3},{2,0},{3,1},{4,6},{5,7},{6,4},{7,5},{8,10},{9,11},{10,... | collective-permute-start | bytes 6488072 | tf_op jit(solution)/shard_map/ppermute | solution.py:33
  30.6 3.5 %collective-permute-start.2 = (bf16[256,2048]{1,0:T(8,128)(2,1)S(1)}, bf16[256,2048]{1,0:T(8,128)(2,1)}, u32[]{:S(2)}, u32[]{:S(2)}) collective-permute-start(bf16[256,2048]{1,0:T(8,128)(2,1)S(1)} %collective-permute-done.refs_3_.refs_2_), channel_id=1, source_target_pairs={{0,1},{1,0},{2,3},{3,2},{4,5},{5,4},{6,7},{7,6},{8,9},{9,8},{10,11... | collective-permute-start | bytes 3145736 | tf_op jit(solution)/shard_map/ppermute | solution.py:33
  30.6 17.8 %collective-permute-start.7 = (bf16[256,1920]{1,0:T(8,128)(2,1)}, bf16[256,1920]{1,0:T(8,128)(2,1)}, u32[]{:S(2)}, u32[]{:S(2)}) collective-permute-start(bf16[256,1920]{1,0:T(8,128)(2,1)} %get-tuple-element.109.refs_0_), channel_id=1, source_target_pairs={{0,1},{1,0},{2,3},{3,2},{4,5},{5,4},{6,7},{7,6},{8,9},{9,8},{10,11... | collective-permute-start | bytes 2949128 | tf_op jit(solution)/shard_map/ppermute | solution.py:33
  31.2 17.2 %copy-start.2 = (bf16[256,1920]{1,0:T(8,128)(2,1)S(1)}, bf16[256,1920]{1,0:T(8,128)(2,1)}, u32[]{:S(2)}) copy-start(bf16[256,1920]{1,0:T(8,128)(2,1)} %get-tuple-element.109.refs_0_) | copy-start | bytes 2949124
  38.5 11.5 %copy-start.1 = (bf16[256,4224]{1,0:T(8,128)(2,1)S(1)}, bf16[256,4224]{1,0:T(8,128)(2,1)}, u32[]{:S(2)}) copy-start(bf16[256,4224]{1,0:T(8,128)(2,1)} %get-tuple-element.104.refs_0_) | copy-start | bytes 6488068
  38.5 6.5 %collective-permute-start.3 = (bf16[64,1280]{1,0:T(8,128)(2,1)S(1)}, bf16[64,1280]{1,0:T(8,128)(2,1)S(1)}, u32[]{:S(2)}, u32[]{:S(2)}) collective-permute-start(bf16[64,1280]{1,0:T(8,128)(2,1)S(1)} %get-tuple-element.76), channel_id=1, source_target_pairs={{0,4},{4,0},{8,12},{12,8},{16,20},{20,16},{24,28},{28,24},{1,5},{5... | collective-permute-start | bytes 491528 | tf_op jit(solution)/shard_map/ppermute | solution.py:33
  45.1 7.2 %collective-permute-start.4 = (bf16[64,1280]{1,0:T(8,128)(2,1)S(1)}, bf16[64,1280]{1,0:T(8,128)(2,1)S(1)}, u32[]{:S(2)}, u32[]{:S(2)}) collective-permute-start(bf16[64,1280]{1,0:T(8,128)(2,1)S(1)} %add_slabs.6.a_ref), channel_id=1, source_target_pairs={{0,8},{4,12},{8,0},{12,4},{16,24},{20,28},{24,16},{28,20},{1,9},{5... | collective-permute-start | bytes 491528 | tf_op jit(solution)/shard_map/ppermute | solution.py:33
  47.0 5.3 %collective-permute-start.5 = (bf16[64,1152]{1,0:T(8,128)(2,1)S(1)}, bf16[64,1152]{1,0:T(8,128)(2,1)S(1)}, u32[]{:S(2)}, u32[]{:S(2)}) collective-permute-start(bf16[64,1152]{1,0:T(8,128)(2,1)S(1)} %get-tuple-element.81), channel_id=1, source_target_pairs={{0,4},{4,0},{8,12},{12,8},{16,20},{20,16},{24,28},{28,24},{1,5},{5... | collective-permute-start | bytes 442376 | tf_op jit(solution)/shard_map/ppermute | solution.py:33
  52.4 10.3 %collective-permute-start.8 = (bf16[64,1280]{1,0:T(8,128)(2,1)S(1)}, bf16[64,1280]{1,0:T(8,128)(2,1)S(1)}, u32[]{:S(2)}, u32[]{:S(2)}) collective-permute-start(bf16[64,1280]{1,0:T(8,128)(2,1)S(1)} %add_slabs.7.a_ref), channel_id=1, source_target_pairs={{0,16},{4,20},{8,24},{12,28},{16,0},{20,4},{24,8},{28,12},{1,17},{... | collective-permute-start | bytes 491528 | tf_op jit(solution)/shard_map/ppermute | solution.py:33
  55.0 7.7 %collective-permute-start.9 = (bf16[64,1152]{1,0:T(8,128)(2,1)S(1)}, bf16[64,1152]{1,0:T(8,128)(2,1)S(1)}, u32[]{:S(2)}, u32[]{:S(2)}) collective-permute-start(bf16[64,1152]{1,0:T(8,128)(2,1)S(1)} %add_slabs.8.a_ref), channel_id=1, source_target_pairs={{0,8},{4,12},{8,0},{12,4},{16,24},{20,28},{24,16},{28,20},{1,9},{5... | collective-permute-start | bytes 442376 | tf_op jit(solution)/shard_map/ppermute | solution.py:33
  62.8 8.4 %collective-permute-start.10 = (bf16[64,1280]{1,0:T(8,128)(2,1)S(1)}, bf16[64,1280]{1,0:T(8,128)(2,1)S(1)}, u32[]{:S(2)}, u32[]{:S(2)}) collective-permute-start(bf16[64,1280]{1,0:T(8,128)(2,1)S(1)} %add_slabs.9.one_ref), channel_id=1, source_target_pairs={{0,4},{4,0},{8,12},{12,8},{16,20},{20,16},{24,28},{28,24},{1,5},{5... | collective-permute-start | bytes 491528 | tf_op jit(solution)/shard_map/ppermute | solution.py:33
  63.7 7.5 %collective-permute-start.11 = (bf16[64,1152]{1,0:T(8,128)(2,1)S(1)}, bf16[64,1152]{1,0:T(8,128)(2,1)S(1)}, u32[]{:S(2)}, u32[]{:S(2)}) collective-permute-start(bf16[64,1152]{1,0:T(8,128)(2,1)S(1)} %add_slabs.10.a_ref), channel_id=1, source_target_pairs={{0,16},{4,20},{8,24},{12,28},{16,0},{20,4},{24,8},{28,12},{1,17},{... | collective-permute-start | bytes 442376 | tf_op jit(solution)/shard_map/ppermute | solution.py:33
  71.3 5.2 %collective-permute-start.12 = (bf16[64,1152]{1,0:T(8,128)(2,1)S(1)}, bf16[64,1152]{1,0:T(8,128)(2,1)S(1)}, u32[]{:S(2)}, u32[]{:S(2)}) collective-permute-start(bf16[64,1152]{1,0:T(8,128)(2,1)S(1)} %add_slabs.11.two_ref), channel_id=1, source_target_pairs={{0,4},{4,0},{8,12},{12,8},{16,20},{20,16},{24,28},{28,24},{1,5},{5... | collective-permute-start | bytes 442376 | tf_op jit(solution)/shard_map/ppermute | solution.py:33
  76.5 5.2 %collective-permute-start.15 = (bf16[256,4224]{1,0:T(8,128)(2,1)}, bf16[256,4224]{1,0:T(8,128)(2,1)S(1)}, u32[]{:S(2)}, u32[]{:S(2)}) collective-permute-start(bf16[256,4224]{1,0:T(8,128)(2,1)} %collective-permute-done.13.refs_2_), channel_id=1, source_target_pairs={{0,1},{1,0},{2,3},{3,2},{4,5},{5,4},{6,7},{7,6},{8,9},{9,8},{10,11... | collective-permute-start | bytes 6488072 | tf_op jit(solution)/shard_map/ppermute | solution.py:33
  76.5 24.2 %collective-permute-start.16 = (bf16[256,1920]{1,0:T(8,128)(2,1)S(1)}, bf16[256,1920]{1,0:T(8,128)(2,1)S(1)}, u32[]{:S(2)}, u32[]{:S(2)}) collective-permute-start(bf16[256,1920]{1,0:T(8,128)(2,1)S(1)} %copy-done.2), channel_id=1, source_target_pairs={{0,2},{1,3},{2,0},{3,1},{4,6},{5,7},{6,4},{7,5},{8,10},{9,11},{10,... | collective-permute-start | bytes 2949128 | tf_op jit(solution)/shard_map/ppermute | solution.py:33
  78.6 3.0 %collective-permute-start.14 = (bf16[256,1280]{1,0:T(8,128)(2,1)S(1)}, bf16[256,1280]{1,0:T(8,128)(2,1)S(1)}, u32[]{:S(2)}, u32[]{:S(2)}) collective-permute-start(bf16[256,1280]{1,0:T(8,128)(2,1)S(1)} %join_slabs.1.refs_1_), channel_id=1, source_target_pairs={{0,1},{1,0},{2,3},{3,2},{4,5},{5,4},{6,7},{7,6},{8,9},{9,8},{10,11... | collective-permute-start | bytes 1966088 | tf_op jit(solution)/shard_map/ppermute | solution.py:33
  100.6 3.4 %collective-permute-start.17 = (bf16[256,1920]{1,0:T(8,128)(2,1)S(1)}, bf16[256,1920]{1,0:T(8,128)(2,1)S(1)}, u32[]{:S(2)}, u32[]{:S(2)}) collective-permute-start(bf16[256,1920]{1,0:T(8,128)(2,1)S(1)} %collective-permute-done.16.refs_2_), channel_id=1, source_target_pairs={{0,1},{1,0},{2,3},{3,2},{4,5},{5,4},{6,7},{7,6},{8,9},{9,8},{10,11... | collective-permute-start | bytes 2949128 | tf_op jit(solution)/shard_map/ppermute | solution.py:33

commit v3 on v2

--- a/solution.py
+++ b/solution.py
@@ -105,7 +105,7 @@
         in_specs=[SMEM, HBM],
         out_specs=(SMEM, VMEM),
         scratch_shapes=[pltpu.SMEM((nblk,), jnp.int32), pltpu.SemaphoreType.DMA],
-        compiler_params=pltpu.CompilerParams(vmem_limit_bytes=60 * MIB),
+        compiler_params=pltpu.CompilerParams(vmem_limit_bytes=50 * MIB),
         name="lead_blocks",
     )(obs_block, ensemble)
 

time: 108 us -> 108 us (level)
  local copies, waits for them, and re-layouts: 0.13 us -> 1.25 us
    unnamed x18 -> x20, local copies, waits for them, and re-layouts: 0.04 us -> 1.16 us
where the time goes in v3:
time: 108 us
  waiting for transfers between devices  46.1 us (43%)
  Pallas kernels  42.8 us (40%)
  starting transfers between devices  16.5 us (15%)
  local copies, waits for them, and re-layouts  1.25 us (1%)
    ppermute x18, waiting for transfers between devices, swap(): return lax.ppermute(x, axis, [(i, i ^ mask) for i in range(size)])  46.1 us
    ppermute x18, starting transfers between devices, swap(): return lax.ppermute(x, axis, [(i, i ^ mask) for i in range(size)])  16.5 us
    pallas_call x3, Pallas kernels, update(): pl.pallas_call(functools.partial(update_kernel, width, parts, start, summ...  12.5 us
    pallas_call x1, Pallas kernels, transform_rows(): pl.pallas_call(functools.partial(root_kernel, parts, scale_root, tile), o...  12.4 us
    pallas_call x3, Pallas kernels, sums(): pl.pallas_call(functools.partial(sums_kernel, width), out_shape=jax.Shape...  5.62 us
    pallas_call x1, Pallas kernels, rest_blocks(): pl.pallas_call(functools.partial(rest_kernel, lead), out_shape=[jax.Shape...  4.42 us
    pallas_call x1, Pallas kernels, gram_rows(): pl.pallas_call(functools.partial(gram_kernel, parts, scale_root, width),...  4.34 us
    pallas_call x1, Pallas kernels, lead_blocks(): pl.pallas_call(lead_kernel, out_shape=(jax.ShapeDtypeStruct((2 * nblk,),...  2.59 us
  transfers between devices with their start and end apart: 18, of which 9 were waited for; matrix products, arithmetic and copies ran while one was open for 1% of the time, Pallas kernels for 34%

profile of v3, /device:TPU:0, one launch (start us, length us, event | category | flops | bytes accessed | tf_op | source)
XLA Modules:
  0.0 107.7 jit_solution(1479754275334881830)
XLA Ops:
  0.0 0.7 copy-done.4
  0.7 2.6 %lead_blocks.1 = (s32[128]{0:T(128)S(1)}, bf16[256,2048]{1,0:T(8,128)(2,1)S(1)}) custom-call(s32[16]{0:T(128)S(1)} %copy-done.4, bf16[256,8192]{1,0:T(8,128)(2,1)} %ens_ref.3), custom_call_target="tpu_custom_call" | custom-call | tf_op jit(solution)/shard_map/lead_blocks/pallas_call | solution.py:99
  3.3 0.5 copy-done.2
  3.8 3.0 %collective-permute-start = (bf16[256,2048]{1,0:T(8,128)(2,1)S(1)}, bf16[256,2048]{1,0:T(8,128)(2,1)S(1)}, u32[]{:S(2)}, u32[]{:S(2)}) collective-permute-start(bf16[256,2048]{1,0:T(8,128)(2,1)S(1)} %get-tuple-element.64.refs_1_.refs_0_), channel_id=1, source_target_pairs={{0,2},{1,3},{2,0},{3,1},{4,6},{5,7},{6,4},{7,5},{8,10},{9,11},{10,... | collective-permute-start | bytes 3145736 | tf_op jit(solution)/shard_map/ppermute | solution.py:33
  6.7 4.4 %rest_blocks.1 = (bf16[256,4224]{1,0:T(8,128)(2,1)}, bf16[256,1920]{1,0:T(8,128)(2,1)}) custom-call(s32[128]{0:T(128)} %copy-done.2, bf16[256,8192]{1,0:T(8,128)(2,1)} %ens_ref.3), custom_call_target="tpu_custom_call" | custom-call | tf_op jit(solution)/shard_map/rest_blocks/pallas_call | solution.py:126
  11.2 0.5 collective-permute-start.6
  11.7 0.0 collective-permute-start.13
  11.7 0.1 broadcast_compare_fusion
  11.8 0.1 select_reduce_fusion
  12.0 0.2 select_reduce_fusion.3
  12.2 0.2 select_reduce_fusion.2
  12.3 18.4 %collective-permute-done.refs_3_.refs_2_ = bf16[256,2048]{1,0:T(8,128)(2,1)S(1)} collective-permute-done((bf16[256,2048]{1,0:T(8,128)(2,1)S(1)}, bf16[256,2048]{1,0:T(8,128)(2,1)S(1)}, u32[]{:S(2)}, u32[]{:S(2)}) %collective-permute-start) | collective-permute-done | bytes 1048608 | tf_op jit(solution)/shard_map/ppermute | solution.py:33
  30.7 0.0 collective-permute-done.1.refs_2_.refs_1_
  30.7 0.1 broadcast_in_dim.73
  30.8 0.0 collective-permute-start.2
  30.8 0.5 collective-permute-start.7
  31.3 0.1 pad_add_fusion.refs_0_.index_ref
  31.4 2.9 %collective-permute-done.2.refs_4_.refs_3_ = bf16[256,2048]{1,0:T(8,128)(2,1)} collective-permute-done((bf16[256,2048]{1,0:T(8,128)(2,1)S(1)}, bf16[256,2048]{1,0:T(8,128)(2,1)}, u32[]{:S(2)}, u32[]{:S(2)}) %collective-permute-start.2) | collective-permute-done | bytes 1048608 | tf_op jit(solution)/shard_map/ppermute | solution.py:33
  34.3 4.3 %gram_rows.1 = (bf16[64,1280]{1,0:T(8,128)(2,1)S(1)}, bf16[64,1280]{1,0:T(8,128)(2,1)S(1)}, bf16[64,1152]{1,0:T(8,128)(2,1)S(1)}, bf16[64,1152]{1,0:T(8,128)(2,1)S(1)}) custom-call(s32[2]{0:T(128)S(1)} %pad_add_fusion.refs_0_.index_ref, bf16[256,2048]{1,0:T(8,128)(2,1)S(1)} %get-tuple-element.64.refs_1_.refs_0_, ...), custom_call_target="tpu_custom_call" | custom-call | flops 1024 | bytes 1024 | tf_op jit(solution)/shard_map/gram_rows/pallas_call | solution.py:246
  38.6 0.0 copy-start
  38.6 2.1 %collective-permute-start.3 = (bf16[64,1280]{1,0:T(8,128)(2,1)S(1)}, bf16[64,1280]{1,0:T(8,128)(2,1)S(1)}, u32[]{:S(2)}, u32[]{:S(2)}) collective-permute-start(bf16[64,1280]{1,0:T(8,128)(2,1)S(1)} %get-tuple-element.76), channel_id=1, source_target_pairs={{0,4},{4,0},{8,12},{12,8},{16,20},{20,16},{24,28},{28,24},{1,5},{5... | collective-permute-start | bytes 491528 | tf_op jit(solution)/shard_map/ppermute | solution.py:33
  40.7 1.8 %sums.3.refs_4_ = f32[1,2048]{1,0:T(1,128)S(1)} custom-call(bf16[256,2048]{1,0:T(8,128)(2,1)S(1)} %get-tuple-element.64.refs_1_.refs_0_, bf16[256,2048]{1,0:T(8,128)(2,1)S(1)} %collective-permute-done.1.refs_2_.refs_1_, bf16[256,2048]{1,0:T(8,128)(2,1)S(1)} %collective-permute-done.refs_3_.refs_2_, bf16[256,2048]{1,0:T(8,128)(2,1)} %collective-permute-done.2.refs_4_.refs_3_), custom_call_target="tpu_custom_call" | custom-call | flops 1024 | bytes 1024 | tf_op jit(solution)/shard_map/sums/pallas_call | solution.py:502
  42.6 2.6 %collective-permute-done.3.b_ref = bf16[64,1280]{1,0:T(8,128)(2,1)S(1)} collective-permute-done((bf16[64,1280]{1,0:T(8,128)(2,1)S(1)}, bf16[64,1280]{1,0:T(8,128)(2,1)S(1)}, u32[]{:S(2)}, u32[]{:S(2)}) %collective-permute-start.3) | collective-permute-done | bytes 163872 | tf_op jit(solution)/shard_map/ppermute | solution.py:33
  45.2 1.9 %collective-permute-start.4 = (bf16[64,1280]{1,0:T(8,128)(2,1)S(1)}, bf16[64,1280]{1,0:T(8,128)(2,1)S(1)}, u32[]{:S(2)}, u32[]{:S(2)}) collective-permute-start(bf16[64,1280]{1,0:T(8,128)(2,1)S(1)} %add_slabs.6.a_ref), channel_id=1, source_target_pairs={{0,8},{4,12},{8,0},{12,4},{16,24},{20,28},{24,16},{28,20},{1,9},{5... | collective-permute-start | bytes 491528 | tf_op jit(solution)/shard_map/ppermute | solution.py:33
  47.1 1.5 %collective-permute-start.5 = (bf16[64,1152]{1,0:T(8,128)(2,1)S(1)}, bf16[64,1152]{1,0:T(8,128)(2,1)S(1)}, u32[]{:S(2)}, u32[]{:S(2)}) collective-permute-start(bf16[64,1152]{1,0:T(8,128)(2,1)S(1)} %get-tuple-element.81), channel_id=1, source_target_pairs={{0,4},{4,0},{8,12},{12,8},{16,20},{20,16},{24,28},{28,24},{1,5},{5... | collective-permute-start | bytes 442376 | tf_op jit(solution)/shard_map/ppermute | solution.py:33
  48.6 0.0 collective-permute-done.7.refs_1_
  48.6 1.5 %sums.5.refs_4_ = f32[1,1920]{1,0:T(1,128)S(1)} custom-call(bf16[256,1920]{1,0:T(8,128)(2,1)S(1)} %copy-done.1, bf16[256,1920]{1,0:T(8,128)(2,1)} %collective-permute-done.7.refs_1_), custom_call_target="tpu_custom_call" | custom-call | flops 1024 | bytes 1024 | tf_op jit(solution)/shard_map/sums/pallas_call | solution.py:502
  50.1 0.0 collective-permute-done.6.refs_1_
  50.1 2.3 %sums.4.refs_4_ = f32[1,4224]{1,0:T(1,128)S(1)} custom-call(bf16[256,4224]{1,0:T(8,128)(2,1)S(1)} %copy-done, bf16[256,4224]{1,0:T(8,128)(2,1)} %collective-permute-done.6.refs_1_), custom_call_target="tpu_custom_call" | custom-call | flops 1024 | bytes 1024 | tf_op jit(solution)/shard_map/sums/pallas_call | solution.py:502
  52.4 0.0 collective-permute-done.4.b_ref
  52.5 2.6 %collective-permute-start.8 = (bf16[64,1280]{1,0:T(8,128)(2,1)S(1)}, bf16[64,1280]{1,0:T(8,128)(2,1)S(1)}, u32[]{:S(2)}, u32[]{:S(2)}) collective-permute-start(bf16[64,1280]{1,0:T(8,128)(2,1)S(1)} %add_slabs.7.a_ref), channel_id=1, source_target_pairs={{0,16},{4,20},{8,24},{12,28},{16,0},{20,4},{24,8},{28,12},{1,17},{... | collective-permute-start | bytes 491528 | tf_op jit(solution)/shard_map/ppermute | solution.py:33
  55.2 0.5 collective-permute-start.9
  55.6 7.2 %collective-permute-done.9.b_ref = bf16[64,1152]{1,0:T(8,128)(2,1)S(1)} collective-permute-done((bf16[64,1152]{1,0:T(8,128)(2,1)S(1)}, bf16[64,1152]{1,0:T(8,128)(2,1)S(1)}, u32[]{:S(2)}, u32[]{:S(2)}) %collective-permute-start.9) | collective-permute-done | bytes 147488 | tf_op jit(solution)/shard_map/ppermute | solution.py:33
  62.8 0.0 collective-permute-done.8.b_ref
  62.9 0.9 collective-permute-start.10
  63.8 7.5 %collective-permute-done.11.b_ref = bf16[64,1152]{1,0:T(8,128)(2,1)S(1)} collective-permute-done((bf16[64,1152]{1,0:T(8,128)(2,1)S(1)}, bf16[64,1152]{1,0:T(8,128)(2,1)S(1)}, u32[]{:S(2)}, u32[]{:S(2)}) %collective-permute-start.11) | collective-permute-done | bytes 147488 | tf_op jit(solution)/shard_map/ppermute | solution.py:33
  71.4 1.2 %collective-permute-start.12 = (bf16[64,1152]{1,0:T(8,128)(2,1)S(1)}, bf16[64,1152]{1,0:T(8,128)(2,1)S(1)}, u32[]{:S(2)}, u32[]{:S(2)}) collective-permute-start(bf16[64,1152]{1,0:T(8,128)(2,1)S(1)} %add_slabs.11.two_ref), channel_id=1, source_target_pairs={{0,4},{4,0},{8,12},{12,8},{16,20},{20,16},{24,28},{28,24},{1,5},{5... | collective-permute-start | bytes 442376 | tf_op jit(solution)/shard_map/ppermute | solution.py:33
  72.6 3.7 %collective-permute-done.13.refs_2_ = bf16[256,4224]{1,0:T(8,128)(2,1)} collective-permute-done((bf16[256,4224]{1,0:T(8,128)(2,1)}, bf16[256,4224]{1,0:T(8,128)(2,1)}, u32[]{:S(2)}, u32[]{:S(2)}) %collective-permute-start.13) | collective-permute-done | bytes 2162720 | tf_op jit(solution)/shard_map/ppermute | solution.py:33
  76.3 0.3 collective-permute-done.12.other_two_ref
  76.6 1.5 %collective-permute-start.16 = (bf16[256,1920]{1,0:T(8,128)(2,1)S(1)}, bf16[256,1920]{1,0:T(8,128)(2,1)S(1)}, u32[]{:S(2)}, u32[]{:S(2)}) collective-permute-start(bf16[256,1920]{1,0:T(8,128)(2,1)S(1)} %copy-done.1), channel_id=1, source_target_pairs={{0,2},{1,3},{2,0},{3,1},{4,6},{5,7},{6,4},{7,5},{8,10},{9,11},{10,... | collective-permute-start | bytes 2949128 | tf_op jit(solution)/shard_map/ppermute | solution.py:33
  78.2 0.6 join_slabs.1.refs_1_
  78.8 0.3 collective-permute-start.14
  79.1 2.8 %collective-permute-done.14.refs_2_ = bf16[256,1280]{1,0:T(8,128)(2,1)S(1)} collective-permute-done((bf16[256,1280]{1,0:T(8,128)(2,1)S(1)}, bf16[256,1280]{1,0:T(8,128)(2,1)S(1)}, u32[]{:S(2)}, u32[]{:S(2)}) %collective-permute-start.14) | collective-permute-done | bytes 655392 | tf_op jit(solution)/shard_map/ppermute | solution.py:33
  81.8 12.4 %transform_rows.1 = (bf16[256,1024]{1,0:T(8,128)(2,1)S(1)}, f32[256,128]{1,0:T(8,128)S(1)}) custom-call(s32[2]{0:T(128)S(1)} %pad_add_fusion.refs_0_.index_ref, bf16[256,1280]{1,0:T(8,128)(2,1)S(1)} %join_slabs.1.refs_1_, bf16[256,1280]{1,0:T(8,128)(2,1)S(1)} %collective-permute-done.14.refs_2_), custom_call_target="tpu_custom_call" | custom-call | flops 1024 | bytes 1024 | tf_op jit(solution)/shard_map/transform_rows/pallas_call | solution.py:471
  94.2 5.8 %update.3.refs_5_ = bf16[256,8192]{1,0:T(8,128)(2,1)} custom-call(s32[128]{0:T(128)S(1)} %copy-done.3, bf16[256,1024]{1,0:T(8,128)(2,1)S(1)} %get-tuple-element.102.t_ref, f32[256,128]{1,0:T(8,128)S(1)} %get-tuple-element.103.rows_ref, f32[1,8192]{1,0:T(1,128)S(1)} %bitcast.12, bf16[256,4224]{1,0:T(8,128)(2,1)S(1)} %copy-done, ...), custom_call_target="tpu_custom_call" | custom-call | flops 1024 | bytes 1024 | tf_op jit(solution)/shard_map/update/pallas_call | solution.py:554
  100.1 0.7 collective-permute-done.16.refs_2_
  100.8 3.4 %update.4.refs_5_ = bf16[256,8192]{1,0:T(8,128)(2,1)} custom-call(s32[128]{0:T(128)S(1)} %copy-done.3, bf16[256,1024]{1,0:T(8,128)(2,1)S(1)} %get-tuple-element.102.t_ref, f32[256,128]{1,0:T(8,128)S(1)} %get-tuple-element.103.rows_ref, f32[1,8192]{1,0:T(1,128)S(1)} %bitcast.13, ...), custom_call_target="tpu_custom_call", output_to_operand_aliasing={{}: (9, {})} | custom-call | flops 1024 | bytes 1024 | tf_op jit(solution)/shard_map/update/pallas_call | solution.py:554
  104.2 3.3 %update.5 = bf16[256,8192]{1,0:T(8,128)(2,1)} custom-call(s32[128]{0:T(128)S(1)} %copy-done.3, bf16[256,1024]{1,0:T(8,128)(2,1)S(1)} %get-tuple-element.102.t_ref, f32[256,128]{1,0:T(8,128)S(1)} %get-tuple-element.103.rows_ref, f32[1,8192]{1,0:T(1,128)S(1)} %bitcast.14, bf16[256,1920]{1,0:T(8,128)(2,1)S(1)} %copy-done.1, ...), custom_call_target="tpu_custom_call", output_to_operand_aliasing={{}: (9, {})} | custom-call | flops 1024 | bytes 1024 | tf_op jit(solution)/shard_map/update/pallas_call | solution.py:554
  (34 shorter events, 0.3 us)
Async XLA Ops:
  0.0 0.7 copy-start.4
  0.7 11.0 %copy-start.6 = (f32[2048]{0:T(1024)S(1)}, f32[2048]{0:T(1024)}, u32[]{:S(2)}) copy-start(f32[2048]{0:T(1024)} %param.11) | copy-start | bytes 24580
  0.7 11.0 %copy-start.7 = (f32[2048]{0:T(1024)S(1)}, f32[2048]{0:T(1024)}, u32[]{:S(2)}) copy-start(f32[2048]{0:T(1024)} %param.10) | copy-start | bytes 24580
  0.7 11.0 %copy-start.5 = (s32[16]{0:T(128)S(1)}, s32[16]{0:T(128)}, u32[]{:S(2)}) copy-start(s32[16]{0:T(128)} %obs_ref.1) | copy-start | bytes 196
  0.7 11.3 %copy-start.8 = (s32[64]{0:T(128)S(1)}, s32[64]{0:T(128)}, u32[]{:S(2)}) copy-start(s32[64]{0:T(128)} %param.7) | copy-start | bytes 772
  0.7 11.5 %copy-start.9 = (f32[64]{0:T(128)S(1)}, f32[64]{0:T(128)}, u32[]{:S(2)}) copy-start(f32[64]{0:T(128)} %param.8) | copy-start | bytes 772
  3.3 0.5 copy-start.2
  3.8 27.0 %collective-permute-start = (bf16[256,2048]{1,0:T(8,128)(2,1)S(1)}, bf16[256,2048]{1,0:T(8,128)(2,1)S(1)}, u32[]{:S(2)}, u32[]{:S(2)}) collective-permute-start(bf16[256,2048]{1,0:T(8,128)(2,1)S(1)} %get-tuple-element.64.refs_1_.refs_0_), channel_id=1, source_target_pairs={{0,2},{1,3},{2,0},{3,1},{4,6},{5,7},{6,4},{7,5},{8,10},{9,11},{10,... | collective-permute-start | bytes 3145736 | tf_op jit(solution)/shard_map/ppermute | solution.py:33
  6.7 5.0 %copy-start.3 = (s32[128]{0:T(128)S(1)}, s32[128]{0:T(128)}, u32[]{:S(2)}) copy-start(s32[128]{0:T(128)} %copy-done.2) | copy-start | bytes 1540
  6.7 24.0 %collective-permute-start.1 = (bf16[256,2048]{1,0:T(8,128)(2,1)S(1)}, bf16[256,2048]{1,0:T(8,128)(2,1)S(1)}, u32[]{:S(2)}, u32[]{:S(2)}) collective-permute-start(bf16[256,2048]{1,0:T(8,128)(2,1)S(1)} %get-tuple-element.64.refs_1_.refs_0_), channel_id=1, source_target_pairs={{0,1},{1,0},{2,3},{3,2},{4,5},{5,4},{6,7},{7,6},{8,9},{9,8},{10,11... | collective-permute-start | bytes 3145736 | tf_op jit(solution)/shard_map/ppermute | solution.py:33
  11.2 39.0 %collective-permute-start.6 = (bf16[256,4224]{1,0:T(8,128)(2,1)}, bf16[256,4224]{1,0:T(8,128)(2,1)}, u32[]{:S(2)}, u32[]{:S(2)}) collective-permute-start(bf16[256,4224]{1,0:T(8,128)(2,1)} %get-tuple-element.104.refs_0_), channel_id=1, source_target_pairs={{0,1},{1,0},{2,3},{3,2},{4,5},{5,4},{6,7},{7,6},{8,9},{9,8},{10,11... | collective-permute-start | bytes 6488072 | tf_op jit(solution)/shard_map/ppermute | solution.py:33
  11.7 64.7 %collective-permute-start.13 = (bf16[256,4224]{1,0:T(8,128)(2,1)}, bf16[256,4224]{1,0:T(8,128)(2,1)}, u32[]{:S(2)}, u32[]{:S(2)}) collective-permute-start(bf16[256,4224]{1,0:T(8,128)(2,1)} %get-tuple-element.104.refs_0_), channel_id=1, source_target_pairs={{0,2},{1,3},{2,0},{3,1},{4,6},{5,7},{6,4},{7,5},{8,10},{9,11},{10,... | collective-permute-start | bytes 6488072 | tf_op jit(solution)/shard_map/ppermute | solution.py:33
  30.8 3.5 %collective-permute-start.2 = (bf16[256,2048]{1,0:T(8,128)(2,1)S(1)}, bf16[256,2048]{1,0:T(8,128)(2,1)}, u32[]{:S(2)}, u32[]{:S(2)}) collective-permute-start(bf16[256,2048]{1,0:T(8,128)(2,1)S(1)} %collective-permute-done.refs_3_.refs_2_), channel_id=1, source_target_pairs={{0,1},{1,0},{2,3},{3,2},{4,5},{5,4},{6,7},{7,6},{8,9},{9,8},{10,11... | collective-permute-start | bytes 3145736 | tf_op jit(solution)/shard_map/ppermute | solution.py:33
  30.8 17.8 %collective-permute-start.7 = (bf16[256,1920]{1,0:T(8,128)(2,1)}, bf16[256,1920]{1,0:T(8,128)(2,1)}, u32[]{:S(2)}, u32[]{:S(2)}) collective-permute-start(bf16[256,1920]{1,0:T(8,128)(2,1)} %get-tuple-element.109.refs_0_), channel_id=1, source_target_pairs={{0,1},{1,0},{2,3},{3,2},{4,5},{5,4},{6,7},{7,6},{8,9},{9,8},{10,11... | collective-permute-start | bytes 2949128 | tf_op jit(solution)/shard_map/ppermute | solution.py:33
  31.4 17.2 %copy-start.1 = (bf16[256,1920]{1,0:T(8,128)(2,1)S(1)}, bf16[256,1920]{1,0:T(8,128)(2,1)}, u32[]{:S(2)}) copy-start(bf16[256,1920]{1,0:T(8,128)(2,1)} %get-tuple-element.109.refs_0_) | copy-start | bytes 2949124
  38.6 11.5 %copy-start = (bf16[256,4224]{1,0:T(8,128)(2,1)S(1)}, bf16[256,4224]{1,0:T(8,128)(2,1)}, u32[]{:S(2)}) copy-start(bf16[256,4224]{1,0:T(8,128)(2,1)} %get-tuple-element.104.refs_0_) | copy-start | bytes 6488068
  38.6 6.5 %collective-permute-start.3 = (bf16[64,1280]{1,0:T(8,128)(2,1)S(1)}, bf16[64,1280]{1,0:T(8,128)(2,1)S(1)}, u32[]{:S(2)}, u32[]{:S(2)}) collective-permute-start(bf16[64,1280]{1,0:T(8,128)(2,1)S(1)} %get-tuple-element.76), channel_id=1, source_target_pairs={{0,4},{4,0},{8,12},{12,8},{16,20},{20,16},{24,28},{28,24},{1,5},{5... | collective-permute-start | bytes 491528 | tf_op jit(solution)/shard_map/ppermute | solution.py:33
  45.2 7.2 %collective-permute-start.4 = (bf16[64,1280]{1,0:T(8,128)(2,1)S(1)}, bf16[64,1280]{1,0:T(8,128)(2,1)S(1)}, u32[]{:S(2)}, u32[]{:S(2)}) collective-permute-start(bf16[64,1280]{1,0:T(8,128)(2,1)S(1)} %add_slabs.6.a_ref), channel_id=1, source_target_pairs={{0,8},{4,12},{8,0},{12,4},{16,24},{20,28},{24,16},{28,20},{1,9},{5... | collective-permute-start | bytes 491528 | tf_op jit(solution)/shard_map/ppermute | solution.py:33
  47.1 5.3 %collective-permute-start.5 = (bf16[64,1152]{1,0:T(8,128)(2,1)S(1)}, bf16[64,1152]{1,0:T(8,128)(2,1)S(1)}, u32[]{:S(2)}, u32[]{:S(2)}) collective-permute-start(bf16[64,1152]{1,0:T(8,128)(2,1)S(1)} %get-tuple-element.81), channel_id=1, source_target_pairs={{0,4},{4,0},{8,12},{12,8},{16,20},{20,16},{24,28},{28,24},{1,5},{5... | collective-permute-start | bytes 442376 | tf_op jit(solution)/shard_map/ppermute | solution.py:33
  52.5 10.3 %collective-permute-start.8 = (bf16[64,1280]{1,0:T(8,128)(2,1)S(1)}, bf16[64,1280]{1,0:T(8,128)(2,1)S(1)}, u32[]{:S(2)}, u32[]{:S(2)}) collective-permute-start(bf16[64,1280]{1,0:T(8,128)(2,1)S(1)} %add_slabs.7.a_ref), channel_id=1, source_target_pairs={{0,16},{4,20},{8,24},{12,28},{16,0},{20,4},{24,8},{28,12},{1,17},{... | collective-permute-start | bytes 491528 | tf_op jit(solution)/shard_map/ppermute | solution.py:33
  55.2 7.7 %collective-permute-start.9 = (bf16[64,1152]{1,0:T(8,128)(2,1)S(1)}, bf16[64,1152]{1,0:T(8,128)(2,1)S(1)}, u32[]{:S(2)}, u32[]{:S(2)}) collective-permute-start(bf16[64,1152]{1,0:T(8,128)(2,1)S(1)} %add_slabs.8.a_ref), channel_id=1, source_target_pairs={{0,8},{4,12},{8,0},{12,4},{16,24},{20,28},{24,16},{28,20},{1,9},{5... | collective-permute-start | bytes 442376 | tf_op jit(solution)/shard_map/ppermute | solution.py:33
  62.9 8.4 %collective-permute-start.10 = (bf16[64,1280]{1,0:T(8,128)(2,1)S(1)}, bf16[64,1280]{1,0:T(8,128)(2,1)S(1)}, u32[]{:S(2)}, u32[]{:S(2)}) collective-permute-start(bf16[64,1280]{1,0:T(8,128)(2,1)S(1)} %add_slabs.9.one_ref), channel_id=1, source_target_pairs={{0,4},{4,0},{8,12},{12,8},{16,20},{20,16},{24,28},{28,24},{1,5},{5... | collective-permute-start | bytes 491528 | tf_op jit(solution)/shard_map/ppermute | solution.py:33
  63.8 7.5 %collective-permute-start.11 = (bf16[64,1152]{1,0:T(8,128)(2,1)S(1)}, bf16[64,1152]{1,0:T(8,128)(2,1)S(1)}, u32[]{:S(2)}, u32[]{:S(2)}) collective-permute-start(bf16[64,1152]{1,0:T(8,128)(2,1)S(1)} %add_slabs.10.a_ref), channel_id=1, source_target_pairs={{0,16},{4,20},{8,24},{12,28},{16,0},{20,4},{24,8},{28,12},{1,17},{... | collective-permute-start | bytes 442376 | tf_op jit(solution)/shard_map/ppermute | solution.py:33
  71.4 5.2 %collective-permute-start.12 = (bf16[64,1152]{1,0:T(8,128)(2,1)S(1)}, bf16[64,1152]{1,0:T(8,128)(2,1)S(1)}, u32[]{:S(2)}, u32[]{:S(2)}) collective-permute-start(bf16[64,1152]{1,0:T(8,128)(2,1)S(1)} %add_slabs.11.two_ref), channel_id=1, source_target_pairs={{0,4},{4,0},{8,12},{12,8},{16,20},{20,16},{24,28},{28,24},{1,5},{5... | collective-permute-start | bytes 442376 | tf_op jit(solution)/shard_map/ppermute | solution.py:33
  76.6 5.2 %collective-permute-start.15 = (bf16[256,4224]{1,0:T(8,128)(2,1)}, bf16[256,4224]{1,0:T(8,128)(2,1)S(1)}, u32[]{:S(2)}, u32[]{:S(2)}) collective-permute-start(bf16[256,4224]{1,0:T(8,128)(2,1)} %collective-permute-done.13.refs_2_), channel_id=1, source_target_pairs={{0,1},{1,0},{2,3},{3,2},{4,5},{5,4},{6,7},{7,6},{8,9},{9,8},{10,11... | collective-permute-start | bytes 6488072 | tf_op jit(solution)/shard_map/ppermute | solution.py:33
  76.6 24.2 %collective-permute-start.16 = (bf16[256,1920]{1,0:T(8,128)(2,1)S(1)}, bf16[256,1920]{1,0:T(8,128)(2,1)S(1)}, u32[]{:S(2)}, u32[]{:S(2)}) collective-permute-start(bf16[256,1920]{1,0:T(8,128)(2,1)S(1)} %copy-done.1), channel_id=1, source_target_pairs={{0,2},{1,3},{2,0},{3,1},{4,6},{5,7},{6,4},{7,5},{8,10},{9,11},{10,... | collective-permute-start | bytes 2949128 | tf_op jit(solution)/shard_map/ppermute | solution.py:33
  78.8 3.0 %collective-permute-start.14 = (bf16[256,1280]{1,0:T(8,128)(2,1)S(1)}, bf16[256,1280]{1,0:T(8,128)(2,1)S(1)}, u32[]{:S(2)}, u32[]{:S(2)}) collective-permute-start(bf16[256,1280]{1,0:T(8,128)(2,1)S(1)} %join_slabs.1.refs_1_), channel_id=1, source_target_pairs={{0,1},{1,0},{2,3},{3,2},{4,5},{5,4},{6,7},{7,6},{8,9},{9,8},{10,11... | collective-permute-start | bytes 1966088 | tf_op jit(solution)/shard_map/ppermute | solution.py:33
  100.8 3.4 %collective-permute-start.17 = (bf16[256,1920]{1,0:T(8,128)(2,1)S(1)}, bf16[256,1920]{1,0:T(8,128)(2,1)S(1)}, u32[]{:S(2)}, u32[]{:S(2)}) collective-permute-start(bf16[256,1920]{1,0:T(8,128)(2,1)S(1)} %collective-permute-done.16.refs_2_), channel_id=1, source_target_pairs={{0,1},{1,0},{2,3},{3,2},{4,5},{5,4},{6,7},{7,6},{8,9},{9,8},{10,11... | collective-permute-start | bytes 2949128 | tf_op jit(solution)/shard_map/ppermute | solution.py:33
